TPU v7x, 512 devices: a whole 4x8x8 slice. The times are simulated.
512 devices in a mesh: dp: 8 (over x, core), mp: 64 (over z, y).
Axes of the slice: x: 4, y: 8, z: 8, core: 2. Of those that a mesh axis runs over, the one named last changes fastest.
Arguments:
- inputs: bfloat16 [1024, 6144], P('dp', 'mp'), may hold values from -6 to 6
- gain: bfloat16 [6144], P('mp'), may hold values from 0.099609375 to 1.8984375
- w_in: bfloat16 [6144, 16384], P('dp', 'mp'), may hold values from -0.078125 to 0.078125
- w_out: bfloat16 [16384, 6144], P('mp', 'dp'), may hold values from -0.046875 to 0.046875
- targets: bfloat16 [1024, 6144], P('dp', 'mp'), may hold values from -7.5 to 7.5
Outputs:
- input_grad: bfloat16 [1024, 6144], P('dp', 'mp')
- gain_grad: float32 [6144], P('mp')
- w_in_grad: float32 [6144, 16384], P('dp', 'mp')
- w_out_grad: float32 [16384, 6144], P('mp', 'dp')
All inputs are finite; a program needn't handle non-finite values.
Results may differ from a plain program's by a relative error of at most 0.0055.
Values may be sent and summed in bfloat16 or wider, within the bound.
A program may use at most 64 MiB of HBM per device.

v0:
```python
import jax
import jax.numpy as jnp
from jax import lax
from jax.sharding import PartitionSpec as P

epsilon = 1e-06


def gelu_value(values):
    return 0.5 * values * (1.0 + jax.scipy.special.erf(values * 0.7071067811865476))


def gelu_slope(values):
    cumul = 0.5 * (1.0 + jax.scipy.special.erf(values * 0.7071067811865476))
    return cumul + values * jnp.exp(-0.5 * values * values) * 0.3989422804014327


def contract_last(left, right):
    return lax.dot_general(
        left, right, (((1,), (1,)), ((), ())), preferred_element_type=jnp.float32
    )


def contract_first(left, right):
    return lax.dot_general(
        left, right, (((0,), (0,)), ((), ())), preferred_element_type=jnp.float32
    )


def shards(inputs, gain, w_in, w_out, targets):
    feat_part = inputs.shape[1]
    feat_width = feat_part * lax.axis_size("mp")
    gain_own = gain.astype(jnp.float32)
    raw_rows = inputs.astype(jnp.float32)
    sum_total, sum_squares = lax.psum(
        (jnp.sum(raw_rows, axis=1), jnp.sum(raw_rows * raw_rows, axis=1)), "mp"
    )
    row_mean = (sum_total / feat_width)[:, None]
    inv_std = lax.rsqrt((sum_squares / feat_width)[:, None] - row_mean * row_mean + epsilon)
    centred = (raw_rows - row_mean) * inv_std
    normed_part = (centred * gain_own).astype(jnp.bfloat16)
    normed = lax.all_gather(normed_part, "mp", axis=1, tiled=True)
    w_in_whole = lax.all_gather(w_in, "dp", axis=0, tiled=True)
    pre_act = jnp.dot(normed, w_in_whole, preferred_element_type=jnp.float32)
    activated = gelu_value(pre_act).astype(jnp.bfloat16)
    targets_whole = lax.all_gather(targets, "mp", axis=1, tiled=True)
    normed_rows, target_rows = (
        lax.all_to_all(normed, "dp", split_axis=1, concat_axis=0, tiled=True),
        lax.all_to_all(targets_whole, "dp", split_axis=1, concat_axis=0, tiled=True),
    )
    act_grad = contract_last(targets_whole, lax.all_gather(w_out, "dp", axis=1, tiled=True))
    pre_grad = (act_grad * gelu_slope(pre_act)).astype(jnp.bfloat16)
    norm_partial = contract_last(pre_grad, w_in_whole)
    norm_grad = lax.psum_scatter(norm_partial, "mp", scatter_dimension=1, tiled=True)
    scaled_grad = norm_grad * gain_own
    first_sum, second = lax.psum(
        (jnp.sum(scaled_grad, axis=1), jnp.sum(scaled_grad * centred, axis=1)), "mp"
    )
    first_mean = (first_sum / feat_width)[:, None]
    second_mean = (second / feat_width)[:, None]
    input_grad = (
        targets.astype(jnp.float32) + inv_std * (scaled_grad - first_mean - centred * second_mean)
    ).astype(jnp.bfloat16)
    gain_grad = lax.psum(jnp.sum(norm_grad * centred, axis=0), "dp")
    act_rows, pre_grad_rows = (
        lax.all_gather(activated, "dp", axis=0, tiled=True),
        lax.all_gather(pre_grad, "dp", axis=0, tiled=True),
    )
    w_in_grad = contract_first(normed_rows, pre_grad_rows)
    w_out_grad = contract_first(act_rows, target_rows)
    return (input_grad, gain_grad, w_in_grad, w_out_grad)


def solution(mesh):
    return jax.shard_map(
        shards,
        mesh=mesh,
        in_specs=(P("dp", "mp"), P("mp"), P("dp", "mp"), P("mp", "dp"), P("dp", "mp")),
        out_specs=(P("dp", "mp"), P("mp"), P("dp", "mp"), P("mp", "dp")),
        check_vma=False,
    )
```

profile of v0, /device:TPU:4, one launch (start us, length us, event | category | flops | bytes accessed | tf_op | source)
XLA Modules:
  0.0 797.2 jit_solution(7876008172515657035)
XLA Ops:
  7.2 0.0 all-gather.9.cloned.1.call-start
  7.2 0.8 fusion.5
  8.0 0.7 convert_element_type.23
  8.6 149.9 %all-reduce.1 = (f32[128]{0:T(128)S(1)}, f32[128]{0:T(128)S(1)}) all-reduce(f32[128]{0:T(128)S(1)} %get-tuple-element.8, f32[128]{0:T(128)S(1)} %get-tuple-element.7), channel_id=1, replica_groups=mesh['dp'=8,'mp'=64] {'mp'}, use_global_device_ids=true, to_apply=%region_3.0 | all-reduce | flops 256 | bytes 2048 | tf_op jit(solution)/shard_map/psum | solution.py:35
  158.5 1.4 fusion.11
  160.0 0.0 all-gather.9.cloned.1.call-update
  160.0 0.0 all-gather.11.cloned.1.call-start
  160.0 0.7 all-gather.11.cloned.1.call-update
  160.7 0.0 all-gather.5.cloned.1.call-start
  160.8 0.7 all-gather.5.cloned.1.call-update
  161.5 0.0 all-gather.7.cloned.1.call-start
  161.5 0.5 all-gather.7.cloned.1.call-update
  162.0 0.0 reduce-scatter.2.cloned.1.call-start
  162.1 71.7 %all-gather.9.cloned.1.call-done = bf16[128,6144]{0,1:T(8,128)(2,1)} async-done(((bf16[128,96]{0,1:T(8,128)(2,1)}), bf16[128,6144]{0,1:T(8,128)(2,1)}) %all-gather.9.cloned.1.call-update) | async-done | bytes 1572880 | tf_op jit(solution)/shard_map/all_gather | solution.py:42
  233.8 31.0 %all-gather.11.cloned.1.call-done = bf16[6144,256]{1,0:T(8,128)(2,1)} async-done(((bf16[768,256]{1,0:T(8,128)(2,1)}), bf16[6144,256]{1,0:T(8,128)(2,1)}) %all-gather.11.cloned.1.call-update) | async-done | bytes 3145744 | tf_op jit(solution)/shard_map/all_gather | solution.py:43
  264.8 3.1 multiply_convert_fusion
  267.9 84.1 %all-gather.5.cloned.1.call-done = bf16[128,6144]{0,1:T(8,128)(2,1)} async-done(((bf16[128,96]{0,1:T(8,128)(2,1)}), bf16[128,6144]{0,1:T(8,128)(2,1)}) %all-gather.5.cloned.1.call-update) | async-done | bytes 1572880 | tf_op jit(solution)/shard_map/all_gather | solution.py:46
  352.0 30.9 %all-gather.7.cloned.1.call-done = bf16[256,6144]{1,0:T(8,128)(2,1)} async-done(((bf16[256,768]{1,0:T(8,128)(2,1)}), bf16[256,6144]{1,0:T(8,128)(2,1)}) %all-gather.7.cloned.1.call-update) | async-done | bytes 3145744 | tf_op jit(solution)/shard_map/all_gather | solution.py:51
  382.9 0.0 copy-start
  382.9 3.7 fusion
  386.6 0.0 copy-done
  386.6 2.6 fusion.18
  389.2 0.0 reduce-scatter.2.cloned.1.call-update
  389.3 0.0 copy-start.1
  389.3 5.4 all-to-all-start.1
  394.7 0.0 copy-done.1
  394.7 1.6 copy.10
  396.2 16.8 %all-to-all-done.1 = bf16[128,8,768]{0,2,1:T(8,128)(2,1)S(1)} async-done(((bf16[128,8,768]{0,2,1:T(8,128)(2,1)}), bf16[128,8,768]{0,2,1:T(8,128)(2,1)S(1)}, u32[]{:S(2)}, u32[]{:S(2)}) %all-to-all-start.1) | async-done | bytes 1572896 | tf_op jit(solution)/shard_map/all_to_all | solution.py:49
  413.1 7.4 all-to-all-start
  420.4 0.7 copy.11
  421.2 26.6 %all_gather.22 = bf16[1024,256]{1,0:T(8,128)(2,1)S(1)} all-gather(bf16[128,256]{1,0:T(8,128)(2,1)S(1)} %fusion), channel_id=1, replica_groups=mesh['dp'=8,'mp'=64] {'dp'}, dimensions={0}, use_global_device_ids=true | all-gather | bytes 589824 | tf_op jit(solution)/shard_map/all_gather | solution.py:67
  447.7 13.1 %all_gather.23 = bf16[1024,256]{1,0:T(8,128)(2,1)S(1)} all-gather(bf16[128,256]{1,0:T(8,128)(2,1)S(1)} %get-tuple-element.15), channel_id=1, replica_groups=mesh['dp'=8,'mp'=64] {'dp'}, dimensions={0}, use_global_device_ids=true | all-gather | bytes 589824 | tf_op jit(solution)/shard_map/all_gather | solution.py:66
  460.8 0.0 all-to-all-done
  460.8 2.9 fusion.19
  463.7 0.0 copy-start.2
  463.7 0.0 copy-start.3
  463.7 1.5 fusion.20
  465.2 171.6 %reduce-scatter.2.cloned.1.call-done = f32[128,96]{0,1:T(8,128)} async-done(((f32[128,6144]{0,1:T(8,128)}), f32[128,96]{0,1:T(8,128)}) %reduce-scatter.2.cloned.1.call-update) | async-done | bytes 49168 | tf_op jit(solution)/shard_map/reduce_scatter | solution.py:54
  636.8 0.0 copy-done.2
  636.8 1.0 fusion.17
  637.8 10.7 %psum.39 = f32[96]{0:T(128)} all-reduce(f32[96]{0:T(128)S(1)} %get-tuple-element.4), channel_id=1, replica_groups=mesh['dp'=8,'mp'=64] {'dp'}, use_global_device_ids=true, to_apply=%region_10.0 | all-reduce | flops 96 | bytes 768 | tf_op jit(solution)/shard_map/psum | solution.py:64
  648.5 140.6 %all-reduce = (f32[128]{0:T(128)S(1)}, f32[128]{0:T(128)S(1)}) all-reduce(f32[128]{0:T(128)S(1)} %get-tuple-element.5, f32[128]{0:T(128)S(1)} %get-tuple-element.6), channel_id=1, replica_groups=mesh['dp'=8,'mp'=64] {'mp'}, use_global_device_ids=true, to_apply=%region_8.0 | all-reduce | flops 256 | bytes 2048 | tf_op jit(solution)/shard_map/psum | solution.py:56
  789.1 0.0 copy-done.3
  789.1 1.5 fusion.16
  (2 shorter events, 0.0 us)
Async XLA Ops:
  7.2 226.6 %all-gather.9.cloned.1.call-start = ((), (), s32[]{:S(2)}) async-start(), calls=%async_computation.5 | async-start | bytes 1597440 | tf_op jit(solution)/shard_map/all_gather | solution.py:42
  160.0 104.8 %all-gather.11.cloned.1.call-start = ((), (), s32[]{:S(2)}) async-start(), calls=%async_computation.6 | async-start | bytes 3538944 | tf_op jit(solution)/shard_map/all_gather | solution.py:43
  160.7 191.2 %all-gather.5.cloned.1.call-start = ((), (), s32[]{:S(2)}) async-start(), calls=%async_computation.3 | async-start | bytes 1597440 | tf_op jit(solution)/shard_map/all_gather | solution.py:46
  161.5 221.4 %all-gather.7.cloned.1.call-start = ((), (), s32[]{:S(2)}) async-start(), calls=%async_computation.4 | async-start | bytes 3538944 | tf_op jit(solution)/shard_map/all_gather | solution.py:51
  162.0 474.8 %reduce-scatter.2.cloned.1.call-start = ((), (), s32[]{:S(2)}) async-start(), calls=%async_computation.7 | async-start | bytes 3194880 | tf_op jit(solution)/shard_map/reduce_scatter | solution.py:54
  382.9 3.7 copy-start
  389.3 5.4 copy-start.1
  389.3 23.8 %all-to-all-start.1 = ((bf16[128,8,768]{0,2,1:T(8,128)(2,1)}), bf16[128,8,768]{0,2,1:T(8,128)(2,1)S(1)}, u32[]{:S(2)}, u32[]{:S(2)}) async-start(bf16[128,8,768]{0,2,1:T(8,128)(2,1)} %bitcast.19), calls=%async_computation.2 | async-start | bytes 3145728 | tf_op jit(solution)/shard_map/all_to_all | solution.py:49
  413.1 47.8 %all-to-all-start = ((bf16[128,8,768]{2,0,1:T(8,128)(2,1)}), bf16[128,8,768]{2,0,1:T(8,128)(2,1)}, u32[]{:S(2)}, u32[]{:S(2)}) async-start(bf16[128,8,768]{2,0,1:T(8,128)(2,1)} %copy.10), calls=%async_computation.1 | async-start | bytes 3145728 | tf_op jit(solution)/shard_map/all_to_all | solution.py:48
  463.7 173.1 %copy-start.2 = (bf16[128,96]{0,1:T(8,128)(2,1)S(1)}, bf16[128,96]{0,1:T(8,128)(2,1)}, u32[]{:S(2)}) copy-start(bf16[128,96]{0,1:T(8,128)(2,1)} %param.5) | copy-start | bytes 73732
  463.7 325.4 %copy-start.3 = (bf16[128,96]{0,1:T(8,128)(2,1)S(1)}, bf16[128,96]{0,1:T(8,128)(2,1)}, u32[]{:S(2)}) copy-start(bf16[128,96]{0,1:T(8,128)(2,1)} %param.9) | copy-start | bytes 73732
Sparse Core Ops, SparseCore 0:
  160.1 73.6 all-gather.8
  235.9 28.8 all-gather.10
  267.8 84.0 all-gather.4
  354.0 28.8 all-gather.6
  389.4 247.3 reduce-scatter.1
where the time goes:
time: 798 us; the launch traced here: 797 us
  waiting for transfers between devices  408 us (51%)
  blocking collectives  341 us (43%)
  matrix products  13.8 us (2%)
  between operations  13.8 us (2%)
  starting transfers between devices  13 us (2%)
    reduce_scatter x1, waiting for transfers between devices, shards(): lax.psum_scatter(norm_partial, 'mp', scatter_dimension=1, tiled=True)  172 us
    psum x1, blocking collectives, shards(): lax.psum((jnp.sum(raw_rows, axis=1), jnp.sum(raw_rows * raw_rows, axis=1)...  150 us
    psum x1, blocking collectives, shards(): lax.psum((jnp.sum(scaled_grad, axis=1), jnp.sum(scaled_grad * centred, ax...  141 us
    all_gather x1, waiting for transfers between devices, shards(): targets_whole = lax.all_gather(targets, 'mp', axis=1, tiled=True)  84.1 us
    all_gather x1, waiting for transfers between devices, shards(): normed = lax.all_gather(normed_part, 'mp', axis=1, tiled=True)  71.7 us
    all_gather x1, waiting for transfers between devices, shards(): w_in_whole = lax.all_gather(w_in, 'dp', axis=0, tiled=True)  31 us
    all_gather x1, waiting for transfers between devices, shards(): lax.all_gather(w_out, 'dp', axis=1, tiled=True)  30.9 us
    all_gather x1, blocking collectives, shards(): lax.all_gather(pre_grad, 'dp', axis=0, tiled=True)  26.6 us
  transfers between devices with their start and end apart: 7, of which 6 were waited for; matrix products, arithmetic and copies ran while one was open for 1% of the time, Pallas kernels for 0%

commit v1 on v0

v1 whole, which is shorter than its diff:
```python
import functools

import jax
import jax.numpy as jnp
from jax import lax
from jax.experimental import pallas as pl
from jax.experimental.pallas import tpu as pltpu
from jax.sharding import PartitionSpec as P

epsilon = 1e-06
MESH = pl.DeviceIdType.MESH
bf16, f32 = jnp.bfloat16, jnp.float32
D = 6144
F = 96
K = 768
H = 256
Q = 32
HALF = F // 2


def gelu_parts(values):
    cumul = 0.5 * (1.0 + lax.erf(values * 0.7071067811865476))
    slope = cumul + values * jnp.exp(-0.5 * values * values) * 0.3989422804014327
    return values * cumul, slope


def turned(rows):
    return jnp.broadcast_to(rows, (128, 128)).T


SCRATCH = dict(
    w1=((K, H), bf16), w2=((H, K), bf16),
    pad=((2, 128, 128), f32), own=((2, F, 128), bf16), gown=((8, 128), f32),
    xg=((8, 8, F, 128), bf16), tg=((8, 8, F, 128), bf16), nt=((8, 8, F, 128), bf16),
    gg=((8, 8, 128), f32), gb=((8, F, 128), f32),
    sta=((8, 8, 128), f32), stb=((8, 8, 128), f32), stc=((8, 8, 128), f32),
    part=((2, 4, 2, Q, 1024), f32), cs=((4, 2, Q, 1024), bf16), cr=((4, 2, Q, 1024), bf16),
    xs=((3, 2, Q, 1024), bf16), xr=((3, 2, Q, 1024), bf16),
    pre=((2, Q, 1024), f32), comb=((8, 2, Q, 1024), bf16),
    u=((8, H), f32), s2p=((8, 8, 128), f32), s2r=((8, 8, 128), f32),
    s2y=((8, 8, 128), f32), s2z=((8, 8, 128), f32),
    ng=((8, 8, F, 128), f32), ra=((2, 2, 4, 8, HALF, 128), bf16), sa=((2, 2, 4, 8, HALF, 128), bf16),
    fs=((2, 8, HALF, 128), bf16), fr=((2, 8, HALF, 128), bf16),
    w1g=((K, H), f32), w2g=((H, K), f32), ge=((8, 8, 128), f32),
)
SEMS = dict(
    loc=(6,), perm=(2, 3), sx=(2, 7), stg=(2, 7), sg=(2, 7), ssa=(2, 7), ssb=(2, 7), ssc=(2, 7),
    ring=(2, 2, 2, 4, 2), core=(2, 4), xx=(2, 3), ax=(2, 3), ac=(2, 4),
    s2a=(2, 7), s2b=(2, 7), s2c=(2, 7), rs=(2, 2, 2, 4, 2), fin=(2, 2, 8), gx=(2, 7),
)


def kernel(x_ref, t_ref, g_ref, w1_hbm, w2_hbm, ig_ref, gg_out, w1g_hbm, w2g_hbm, *scratch):
    S = dict(zip(list(SCRATCH) + list(SEMS), scratch, strict=True))
    d, m = lax.axis_index("dp"), lax.axis_index("mp")
    z, y = m // 8, m % 8
    chip, core = d // 2, d % 2
    diag = d == z
    off_diag = jnp.logical_not(diag)
    sends = []

    def at(dp, zz, yy):
        return (dp, zz * 8 + yy)

    def remote(src, dst, sem, index, dev, landing=None):
        return pltpu.make_async_remote_copy(
            src_ref=src, dst_ref=dst, send_sem=S[sem].at[(0, *index)],
            recv_sem=S[sem].at[(1, *(landing or index))], device_id=dev, device_id_type=MESH)

    def go(src, dst, sem, index, dev):
        copy = remote(src, dst, sem, index, dev)
        copy.start()
        sends.append(copy)
        return copy

    def along(axis, i):
        if axis == "dp":
            return at((d + i) % 8, z, y)
        if axis == "z":
            return at(d, (z + i) % 8, y)
        return at(d, z, (y + i) % 8)

    def spread(buf, slot, sem, axis):
        return [go(S[buf].at[slot], S[buf].at[slot], sem, (i - 1,), along(axis, i)) for i in range(1, 8)]

    def arrive(copies):
        for copy in copies:
            copy.wait_recv()

    load1 = pltpu.make_async_copy(w1_hbm, S["w1"], S["loc"].at[0])
    load2 = pltpu.make_async_copy(w2_hbm, S["w2"], S["loc"].at[1])
    load1.start()
    load2.start()

    barrier = pltpu.get_barrier_semaphore()

    def hail(dev):
        pl.semaphore_signal(barrier, inc=1, device_id=dev, device_id_type=MESH)

    for axis in ("dp", "z", "y"):
        for i in range(1, 8):
            hail(along(axis, i))

    @pl.when(off_diag)
    def _():
        for i in range(1, 8):
            hail(at((d + i) % 8, d, y))
            hail(at(z, (z + i) % 8, y))
            hail(at(z, d, (y + i) % 8))

    S["pad"][...] = jnp.zeros_like(S["pad"])
    S["pad"][0, :, :F] = x_ref[...].astype(f32)
    S["pad"][1, :, :F] = t_ref[...].astype(f32)
    for i in range(2):
        S["own"][i] = S["pad"][i].T[:F].astype(bf16)
    S["gown"][...] = jnp.zeros_like(S["gown"])
    S["gown"][:, :F] = jnp.broadcast_to(g_ref[...].astype(f32), (8, F))

    @pl.when(off_diag)
    def _():
        pl.semaphore_wait(barrier, 42)

    @pl.when(diag)
    def _():
        pl.semaphore_wait(barrier, 21)

    perm = [
        (S["own"].at[0], S["xg"].at[d, y], S["xg"].at[z, y]),
        (S["own"].at[1], S["tg"].at[d, y], S["tg"].at[z, y]),
        (S["gown"], S["gg"].at[y], S["gg"].at[y]),
    ]
    perm = [remote(src, dst, "perm", (i,), at(z, d, y)) for i, (src, dst, _) in enumerate(perm)]

    @pl.when(off_diag)
    def _():
        for copy in perm:
            copy.start()

    @pl.when(diag)
    def _():
        pltpu.make_async_copy(S["own"].at[0], S["xg"].at[z, y], S["perm"].at[1, 0]).start()
        pltpu.make_async_copy(S["own"].at[1], S["tg"].at[z, y], S["perm"].at[1, 1]).start()
        pltpu.make_async_copy(S["gown"], S["gg"].at[y], S["perm"].at[1, 2]).start()

    arrive(perm)

    gx = [
        go(S["xg"].at[z, y], S["xg"].at[z, y], "sx", (i - 1,), along("z", i)) for i in range(1, 8)]
    gt = [go(S["tg"].at[z, y], S["tg"].at[z, y], "stg", (i - 1,), along("y", i)) for i in range(1, 8)]
    ggain = spread("gg", y, "sg", "y")
    piece = S["xg"][z, y].astype(f32)
    S["sta"][y] = jnp.zeros((8, 128), f32)
    S["sta"][y, 0:1] = jnp.sum(piece, axis=0, keepdims=True)
    S["sta"][y, 1:2] = jnp.sum(piece * piece, axis=0, keepdims=True)
    sta = spread("sta", y, "ssa", "y")
    arrive(gx)
    arrive(gt)

    def ring_ref(axis, origin, sub):
        half = pl.ds(4 * sub, 4)
        if axis == 0:
            return S["xg"].at[half, origin]
        return S["tg"].at[origin, half]

    ring = {}

    def ring_step(k):
        for sub in (0, 1):
            for axis in (0, 1):
                for way in (0, 1):
                    if k == 4 and sub != way:
                        continue
                    sign = 1 - 2 * way
                    me = y if axis == 0 else z
                    if k > 1:
                        ring[axis, way, k - 1, sub].wait_recv()
                    ref = ring_ref(axis, (me - sign * (k - 1) + 8) % 8, sub)
                    ring[axis, way, k, sub] = go(
                        ref, ref, "ring", (axis, way, k - 1, sub), along("yz"[axis], sign + 8))

    ring_step(1)
    arrive(sta)
    S["stb"][d] = jnp.sum(S["sta"][...], axis=0)
    stb = spread("stb", d, "ssb", "dp")
    arrive(ggain)
    load1.wait()
    load2.wait()
    total = jnp.zeros((8, H), f32)
    for i in range(8):
        rows = S["gg"][i]
        S["gb"][i] = turned(rows[0:1])[:F]
        total += jnp.dot(rows[:, :F].astype(bf16), S["w1"][F * i:F * (i + 1)], preferred_element_type=f32)
    S["u"][...] = total
    ring_step(2)
    arrive(stb)
    S["stc"][z] = jnp.sum(S["stb"][...], axis=0)
    stc = spread("stc", z, "ssc", "z")
    ring_step(3)
    arrive(stc)
    ring_step(4)
    for axis in (0, 1):
        for way in (0, 1):
            ring[axis, way, 3, 1 - way].wait_recv()
            ring[axis, way, 4, way].wait_recv()

    def scale_of(tile):
        mean = tile[0:1] / D
        return mean, lax.rsqrt(tile[1:2] / D - mean * mean + epsilon)

    def normed(tok, carry):
        mean, inv = scale_of(S["stc"][tok])
        for i in range(8):
            S["nt"][tok, i] = ((S["xg"][tok, i].astype(f32) - mean) * inv * S["gb"][i]).astype(bf16)
        return carry

    lax.fori_loop(0, 8, normed, 0)

    def pair(ref, i):
        return jnp.concatenate(
            [ref[2 * i].reshape(K, 128), ref[2 * i + 1].reshape(K, 128)], axis=1)

    for i in range(4):
        lanes = slice(256 * i, 256 * (i + 1))
        pre_part = lax.dot_general(
            S["w1"][...], pair(S["nt"], i), (((0,), (0,)), ((), ())), preferred_element_type=f32)
        act_part = jnp.dot(S["w2"][...], pair(S["tg"], i), preferred_element_type=f32)
        S["part"][0, :, :, :, lanes] = pre_part.reshape(4, 2, Q, 256)
        S["part"][1, :, :, :, lanes] = act_part.reshape(4, 2, Q, 256)

    pairs = []
    for i in (1, 2, 3, 0):
        to = (chip + i) % 4
        for arr in range(2):
            S["cs"][to, arr] = S["part"][arr, to, 1 - core].astype(bf16)
        pairs.append(go(S["cs"].at[to], S["cr"].at[to], "core", (i,), at(2 * chip + 1 - core, z, y)))
    hops = []
    for i in (1, 2, 3):
        to = (chip + i) % 4
        pairs[i - 1].wait_recv()
        for arr in range(2):
            S["xs"][i - 1, arr] = (S["part"][arr, to, core] + S["cr"][to, arr].astype(f32)).astype(bf16)
        hops.append(go(S["xs"].at[i - 1], S["xr"].at[i - 1], "xx", (i - 1,), at(2 * to + core, z, y)))
    pairs[3].wait_recv()
    for arr in range(2):
        S["pre"][arr] = S["part"][arr, chip, core] + S["cr"][chip, arr].astype(f32)
    for i in range(3):
        hops[i].wait_recv()
    pre_act = S["pre"][0] + sum(S["xr"][i, 0].astype(f32) for i in range(3))
    act_grad = S["pre"][1] + sum(S["xr"][i, 1].astype(f32) for i in range(3))
    value, slope = gelu_parts(pre_act)
    pre_grad = (act_grad * slope).astype(bf16)
    S["comb"][d, 0] = value.astype(bf16)
    S["comb"][d, 1] = pre_grad
    second = jnp.sum(pre_grad.astype(f32) * pre_act, axis=0, keepdims=True)

    hops = [
        go(S["comb"].at[d], S["comb"].at[d], "ax", (i - 1,), at(2 * ((chip + i) % 4) + core, z, y))
        for i in (1, 2, 3)]
    pairs = []
    for i in (0, 3, 2, 1):
        slot = 2 * ((chip + i) % 4) + core
        if i:
            hops[3 - i].wait_recv()
        pairs.append(go(
            S["comb"].at[slot], S["comb"].at[slot], "ac", (i,), at(2 * chip + 1 - core, z, y)))
    arrive(pairs)

    for i in range(4):
        lanes = slice(256 * i, 256 * (i + 1))
        out = jnp.dot(S["w1"][...], S["comb"][:, 1, :, lanes].reshape(H, 256), preferred_element_type=f32)
        S["ng"][2 * i] = out[:, :128].reshape(8, F, 128)
        S["ng"][2 * i + 1] = out[:, 128:].reshape(8, F, 128)

    rs = {}

    def rs_block(axis, dest, sub):
        half = pl.ds(4 * sub, 4)
        if axis == 0:
            return S["ng"][half, dest, 0:HALF]
        return S["ng"][dest, half, HALF:F]

    def rs_add(axis, way, k, sub, val):
        if (axis, way, k, sub) in rs:
            rs[axis, way, k, sub].wait_recv()
            val = val + S["ra"][axis, way, k - 1, pl.ds(4 * sub, 4)].astype(f32)
        return val

    def rs_step(k):
        for sub in (0, 1):
            for axis in (0, 1):
                for way in (0, 1):
                    if k == 1 and sub != way:
                        continue
                    sign = 1 - 2 * way
                    me = y if axis == 0 else z
                    val = rs_block(axis, (me + sign * (5 - k) + 8) % 8, sub)
                    val = rs_add(axis, way, k - 1, sub, val)
                    half = pl.ds(4 * sub, 4)
                    S["sa"][axis, way, k - 1, half] = val.astype(bf16)
                    rs[axis, way, k, sub] = go(
                        S["sa"].at[axis, way, k - 1, half], S["ra"].at[axis, way, k - 1, half],
                        "rs", (axis, way, k - 1, sub), along("yz"[axis], sign + 8))

    rs_step(1)
    pg = S["comb"][:, 1].reshape(H, 1024)
    high = S["u"][...].astype(bf16)
    low = (S["u"][...] - high.astype(f32)).astype(bf16)
    first = jnp.dot(high, pg, preferred_element_type=f32) + jnp.dot(low, pg, preferred_element_type=f32)
    S["s2p"][...] = jnp.zeros_like(S["s2p"])
    for i in range(8):
        lanes = slice(128 * i, 128 * (i + 1))
        S["s2p"][i, 0:1] = first[0:1, lanes]
        S["s2p"][i, 1:2] = second[:, lanes]
    s2a = [
        go(S["s2p"].at[(d + i) % 8], S["s2r"].at[d], "s2a", (i - 1,), along("dp", i)) for i in range(1, 8)]
    S["s2r"][d] = S["s2p"][d]
    rs_step(2)
    nt_all = jnp.concatenate([S["nt"][i].reshape(K, 128) for i in range(8)], axis=1)
    S["w1g"][...] = lax.dot_general(nt_all, pg, (((1,), (1,)), ((), ())), preferred_element_type=f32)
    store1 = pltpu.make_async_copy(S["w1g"], w1g_hbm, S["loc"].at[2])
    store1.start()
    arrive(s2a)
    S["s2y"][y] = jnp.sum(S["s2r"][...], axis=0)
    s2b = spread("s2y", y, "s2b", "y")
    rs_step(3)
    tg_all = jnp.concatenate([S["tg"][i].reshape(K, 128) for i in range(8)], axis=1)
    S["w2g"][...] = lax.dot_general(
        S["comb"][:, 0].reshape(H, 1024), tg_all, (((1,), (1,)), ((), ())), preferred_element_type=f32)
    store2 = pltpu.make_async_copy(S["w2g"], w2g_hbm, S["loc"].at[3])
    store2.start()
    arrive(s2b)
    S["s2z"][z] = jnp.sum(S["s2y"][...], axis=0)
    s2c = spread("s2z", z, "s2c", "z")
    rs_step(4)
    arrive(s2c)
    for axis in (0, 1):
        for sub in (0, 1):
            half = pl.ds(4 * sub, 4)
            val = rs_block(axis, y if axis == 0 else z, sub)
            for way in (0, 1):
                val = rs_add(axis, way, 4, sub, val)
            S["fs"][axis, half] = val.astype(bf16)

    fins = []
    for axis in (0, 1):
        for i in range(8):
            if axis == 0:
                step = (d + i) % 8
                dev, slot = at(step, d, y), z
                clear = jnp.logical_or(off_diag, step != d)
            else:
                step = (y + i) % 8
                dev, slot = at(z, d, step), y
                clear = jnp.logical_or(off_diag, step != y)
            copy = remote(S["fs"].at[axis, step], S["fr"].at[axis, slot], "fin", (axis, i), dev, (axis, slot))
            if i:
                copy.start()
            else:
                @pl.when(clear)
                def _():
                    copy.start()

                @pl.when(jnp.logical_not(clear))
                def _():
                    pltpu.make_async_copy(
                        S["fs"].at[axis, step], S["fr"].at[axis, slot], S["fin"].at[1, axis, slot]).start()
            fins.append((copy, i, clear))
    gcol = turned(S["gown"][0:1])[:F]
    mean, inv = scale_of(S["stc"][d])
    cen = (S["own"][0].astype(f32) - mean) * inv
    tile = jnp.sum(S["s2z"][...], axis=0)
    base = S["own"][1].astype(f32) - inv * (tile[0:1] / D + cen * (tile[1:2] / D))
    for axis in (0, 1):
        for slot in range(8):
            remote(S["fs"].at[axis, slot], S["fr"].at[axis, slot], "fin", (axis, slot), at(z, d, y)).wait_recv()
        S["pad"][0, HALF * axis:HALF * (axis + 1)] = jnp.sum(S["fr"][axis].astype(f32), axis=0)
    grad = S["pad"][0, :F]
    S["pad"][1, :F] = grad * cen
    S["ge"][d] = jnp.broadcast_to(jnp.sum(S["pad"][1].T, axis=0, keepdims=True), (8, 128))
    ge = spread("ge", d, "gx", "dp")
    S["pad"][0, :F] = base + inv * (grad * gcol)
    ig_ref[...] = S["pad"][0].T[:, :F].astype(bf16)
    arrive(ge)
    gg_out[...] = jnp.sum(S["ge"][...], axis=0)

    for copy in sends:
        copy.wait_send()
    for copy, i, clear in fins:
        if i:
            copy.wait_send()
        else:
            @pl.when(clear)
            def _():
                copy.wait_send()

    @pl.when(off_diag)
    def _():
        for copy in perm:
            copy.wait_send()

    store1.wait()
    store2.wait()


def shards(inputs, gain, w_in, w_out, targets):
    vmem, hbm = pl.BlockSpec(memory_space=pltpu.VMEM), pl.BlockSpec(memory_space=pl.ANY)
    scratch = [pltpu.VMEM(shape, kind) for shape, kind in SCRATCH.values()]
    scratch += [pltpu.SemaphoreType.DMA(shape) for shape in SEMS.values()]
    input_grad, gain_grad, w_in_grad, w_out_grad = pl.pallas_call(
        kernel,
        out_shape=(
            jax.ShapeDtypeStruct((128, F), bf16), jax.ShapeDtypeStruct((8, 128), f32),
            jax.ShapeDtypeStruct((K, H), f32), jax.ShapeDtypeStruct((H, K), f32)),
        in_specs=[vmem, vmem, vmem, hbm, hbm],
        out_specs=(vmem, vmem, hbm, hbm),
        scratch_shapes=scratch,
        compiler_params=pltpu.CompilerParams(
            collective_id=0, has_side_effects=True, vmem_limit_bytes=48 * 1024 * 1024),
        cost_estimate=pl.CostEstimate(flops=2 * 10 ** 9, bytes_accessed=4 * 10 ** 6, transcendentals=10 ** 5),
        name="backward",
    )(inputs, targets, gain.reshape(1, F), w_in, w_out)
    return input_grad, gain_grad[0, :F], w_in_grad, w_out_grad


def solution(mesh):
    return jax.shard_map(
        shards,
        mesh=mesh,
        in_specs=(P("dp", "mp"), P("mp"), P("dp", "mp"), P("mp", "dp"), P("dp", "mp")),
        out_specs=(P("dp", "mp"), P("mp"), P("dp", "mp"), P("mp", "dp")),
        check_vma=False,
    )
```

time: 798 us -> 117 us (0.15)
  the two profiles are of different devices: /device:TPU:4 before, /device:TPU:1 now
where the time goes in v1:
time: 117 us
  Pallas kernels  110 us (94%)
  local copies, waits for them, and re-layouts  6.46 us (6%)
    pallas_call x1, Pallas kernels, shards(): pl.pallas_call(kernel, out_shape=(jax.ShapeDtypeStruct((128, F), bf16), j...  110 us
    unnamed x13, local copies, waits for them, and re-layouts  5.95 us

profile of v1, /device:TPU:1, one launch (start us, length us, event | category | flops | bytes accessed | tf_op | source)
XLA Modules:
  0.0 116.9 jit_solution(12573710655407874601)
XLA Ops:
  0.6 0.0 copy-start.3
  0.6 0.8 copy.9.x_ref
  1.5 0.0 copy-done.3
  1.5 0.0 copy-start.2
  1.5 0.1 copy.10.t_ref
  1.6 0.5 copy-done.2
  2.2 0.0 copy-start
  2.2 1.0 copy-done
  3.2 0.0 copy-start.1
  3.2 1.0 copy-done.1
  4.2 109.8 %backward.1 = (bf16[128,96]{1,0:T(8,128)(2,1)S(1)}, f32[8,128]{1,0:T(8,128)S(1)}, f32[768,256]{1,0:T(8,128)S(1)}, f32[256,768]{1,0:T(8,128)S(1)}) custom-call(bf16[128,96]{1,0:T(8,128)(2,1)S(1)} %copy.9.x_ref, bf16[128,96]{1,0:T(8,128)(2,1)S(1)} %copy.10.t_ref, bf16[1,96]{1,0:T(2,128)(2,1)S(1)} %bitcast.3, bf16[768,256]{1,0:T(8,128)(2,1)S(1)} %copy-done, ...), custom_call_target="tpu_custom_call" | custom-call | flops 2000000000 | bytes 4000000 | tf_op jit(solution)/shard_map/backward/pallas_call | solution.py:409
  113.9 0.7 copy.11
  114.6 0.5 slice_bitcast_fusion
  115.2 0.9 copy.14
  116.0 0.9 copy.15
Async XLA Ops:
  0.6 0.9 copy-start.3
  1.5 0.7 copy-start.2
  2.2 1.0 copy-start
  3.2 1.0 copy-start.1

commit v2 on v1

--- a/solution.py
+++ b/solution.py
@@ -24,13 +24,19 @@
     return values * cumul, slope
 
 
+def when_wait(cond, copy):
+    @pl.when(cond)
+    def _():
+        copy.wait_send()
+
+
 def turned(rows):
     return jnp.broadcast_to(rows, (128, 128)).T
 
 
 SCRATCH = dict(
     w1=((K, H), bf16), w2=((H, K), bf16),
-    pad=((2, 128, 128), f32), own=((2, F, 128), bf16), gown=((8, 128), f32),
+    pad=((128, 128), f32), gown=((8, 128), f32),
     xg=((8, 8, F, 128), bf16), tg=((8, 8, F, 128), bf16), nt=((8, 8, F, 128), bf16),
     gg=((8, 8, 128), f32), gb=((8, F, 128), f32),
     sta=((8, 8, 128), f32), stb=((8, 8, 128), f32), stc=((8, 8, 128), f32),
@@ -44,33 +50,48 @@
     w1g=((K, H), f32), w2g=((H, K), f32), ge=((8, 8, 128), f32),
 )
 SEMS = dict(
-    loc=(6,), perm=(2, 3), sx=(2, 7), stg=(2, 7), sg=(2, 7), ssa=(2, 7), ssb=(2, 7), ssc=(2, 7),
-    ring=(2, 2, 2, 4, 2), core=(2, 4), xx=(2, 3), ax=(2, 3), ac=(2, 4),
-    s2a=(2, 7), s2b=(2, 7), s2c=(2, 7), rs=(2, 2, 2, 4, 2), fin=(2, 2, 8), gx=(2, 7),
+    loc=(4,), perm=(2, 3), sx=(2, 7), stg=(2, 7), small=(2, 10), ring_s=(2, 4), ring_r=(2, 2, 4, 4),
+    core=(2, 4), xx=(2, 3), ax=(2, 3), ac=(2, 4), rs=(2, 2, 2, 4, 2), fin_s=(2, 2), fin_r=(2,),
 )
 
 
-def kernel(x_ref, t_ref, g_ref, w1_hbm, w2_hbm, ig_ref, gg_out, w1g_hbm, w2g_hbm, *scratch):
+LAST = None
+
+
+def kernel(*refs):
+    ends = []
+    for name in phases(ends, *refs):
+        if name == LAST:
+            break
+    for end in ends:
+        end()
+
+
+def phases(ends, x_ref, t_ref, g_ref, w1_hbm, w2_hbm, ig_ref, gg_out, w1g_hbm, w2g_hbm, *scratch):
     S = dict(zip(list(SCRATCH) + list(SEMS), scratch, strict=True))
     d, m = lax.axis_index("dp"), lax.axis_index("mp")
     z, y = m // 8, m % 8
     chip, core = d // 2, d % 2
     diag = d == z
     off_diag = jnp.logical_not(diag)
-    sends = []
 
     def at(dp, zz, yy):
         return (dp, zz * 8 + yy)
 
-    def remote(src, dst, sem, index, dev, landing=None):
+    def remote(src, dst, sem, index, dev):
         return pltpu.make_async_remote_copy(
             src_ref=src, dst_ref=dst, send_sem=S[sem].at[(0, *index)],
-            recv_sem=S[sem].at[(1, *(landing or index))], device_id=dev, device_id_type=MESH)
+            recv_sem=S[sem].at[(1, *index)], device_id=dev, device_id_type=MESH)
+
+    def whole(ref, send_sem, recv_sem):
+        return pltpu.make_async_remote_copy(
+            src_ref=ref, dst_ref=ref, send_sem=send_sem, recv_sem=recv_sem,
+            device_id=at(z, d, y), device_id_type=MESH)
 
     def go(src, dst, sem, index, dev):
         copy = remote(src, dst, sem, index, dev)
         copy.start()
-        sends.append(copy)
+        ends.append(copy.wait_send)
         return copy
 
     def along(axis, i):
@@ -80,8 +101,13 @@
             return at(d, (z + i) % 8, y)
         return at(d, z, (y + i) % 8)
 
-    def spread(buf, slot, sem, axis):
-        return [go(S[buf].at[slot], S[buf].at[slot], sem, (i - 1,), along(axis, i)) for i in range(1, 8)]
+    def spread(buf, slot, number, axis, source=None):
+        for i in range(1, 8):
+            src = S[buf].at[slot] if source is None else source(i)
+            remote(src, S[buf].at[slot], "small", (number,), along(axis, i)).start()
+        seven = whole(S[buf].at[pl.ds(0, 7)], S["small"].at[0, number], S["small"].at[1, number])
+        ends.append(seven.wait_send)
+        return [seven]
 
     def arrive(copies):
         for copy in copies:
@@ -91,6 +117,8 @@
     load2 = pltpu.make_async_copy(w2_hbm, S["w2"], S["loc"].at[1])
     load1.start()
     load2.start()
+    loads = [load1.wait, load2.wait]
+    ends.extend(loads)
 
     barrier = pltpu.get_barrier_semaphore()
 
@@ -103,33 +131,29 @@
 
     @pl.when(off_diag)
     def _():
-        for i in range(1, 8):
-            hail(at((d + i) % 8, d, y))
-            hail(at(z, (z + i) % 8, y))
-            hail(at(z, d, (y + i) % 8))
+        hail(at(z, d, y))
 
     S["pad"][...] = jnp.zeros_like(S["pad"])
-    S["pad"][0, :, :F] = x_ref[...].astype(f32)
-    S["pad"][1, :, :F] = t_ref[...].astype(f32)
-    for i in range(2):
-        S["own"][i] = S["pad"][i].T[:F].astype(bf16)
     S["gown"][...] = jnp.zeros_like(S["gown"])
     S["gown"][:, :F] = jnp.broadcast_to(g_ref[...].astype(f32), (8, F))
 
     @pl.when(off_diag)
     def _():
-        pl.semaphore_wait(barrier, 42)
+        pl.semaphore_wait(barrier, 22)
 
     @pl.when(diag)
     def _():
         pl.semaphore_wait(barrier, 21)
 
+    if LAST == "barrier":
+        return
+
     perm = [
-        (S["own"].at[0], S["xg"].at[d, y], S["xg"].at[z, y]),
-        (S["own"].at[1], S["tg"].at[d, y], S["tg"].at[z, y]),
-        (S["gown"], S["gg"].at[y], S["gg"].at[y]),
+        (x_ref, S["xg"].at[d, y]),
+        (t_ref, S["tg"].at[d, y]),
+        (S["gown"], S["gg"].at[y]),
     ]
-    perm = [remote(src, dst, "perm", (i,), at(z, d, y)) for i, (src, dst, _) in enumerate(perm)]
+    perm = [remote(src, dst, "perm", (i,), at(z, d, y)) for i, (src, dst) in enumerate(perm)]
 
     @pl.when(off_diag)
     def _():
@@ -138,70 +162,105 @@
 
     @pl.when(diag)
     def _():
-        pltpu.make_async_copy(S["own"].at[0], S["xg"].at[z, y], S["perm"].at[1, 0]).start()
-        pltpu.make_async_copy(S["own"].at[1], S["tg"].at[z, y], S["perm"].at[1, 1]).start()
+        pltpu.make_async_copy(x_ref, S["xg"].at[z, y], S["perm"].at[1, 0]).start()
+        pltpu.make_async_copy(t_ref, S["tg"].at[z, y], S["perm"].at[1, 1]).start()
         pltpu.make_async_copy(S["gown"], S["gg"].at[y], S["perm"].at[1, 2]).start()
 
+    @ends.append
+    def _():
+        @pl.when(off_diag)
+        def _():
+            for copy in perm:
+                copy.wait_send()
+
     arrive(perm)
+    yield "permute"
 
     gx = [
         go(S["xg"].at[z, y], S["xg"].at[z, y], "sx", (i - 1,), along("z", i)) for i in range(1, 8)]
     gt = [go(S["tg"].at[z, y], S["tg"].at[z, y], "stg", (i - 1,), along("y", i)) for i in range(1, 8)]
-    ggain = spread("gg", y, "sg", "y")
+    ggain = spread("gg", y, 0, "y")
     piece = S["xg"][z, y].astype(f32)
     S["sta"][y] = jnp.zeros((8, 128), f32)
     S["sta"][y, 0:1] = jnp.sum(piece, axis=0, keepdims=True)
     S["sta"][y, 1:2] = jnp.sum(piece * piece, axis=0, keepdims=True)
-    sta = spread("sta", y, "ssa", "y")
-    arrive(gx)
-    arrive(gt)
-
-    def ring_ref(axis, origin, sub):
-        half = pl.ds(4 * sub, 4)
+    sta = spread("sta", y, 1, "y")
+    def offset(e):
+        return (e + 1) // 2 if e % 2 else (8 - e // 2) % 8
+
+    def ring_piece(axis, origin, e):
+        if isinstance(e, int):
+            off = offset(e)
+        else:
+            off = jnp.where(e % 2 == 1, (e + 1) // 2, (8 - e // 2) % 8)
         if axis == 0:
-            return S["xg"].at[half, origin]
-        return S["tg"].at[origin, half]
-
-    ring = {}
-
-    def ring_step(k):
-        for sub in (0, 1):
-            for axis in (0, 1):
-                for way in (0, 1):
-                    if k == 4 and sub != way:
-                        continue
-                    sign = 1 - 2 * way
-                    me = y if axis == 0 else z
-                    if k > 1:
-                        ring[axis, way, k - 1, sub].wait_recv()
-                    ref = ring_ref(axis, (me - sign * (k - 1) + 8) % 8, sub)
-                    ring[axis, way, k, sub] = go(
-                        ref, ref, "ring", (axis, way, k - 1, sub), along("yz"[axis], sign + 8))
-
-    ring_step(1)
+            return S["xg"].at[(z + off) % 8, origin]
+        return S["tg"].at[origin, (y + off) % 8]
+
+    def ring_send(axis, way, k, j, p):
+        sign = 1 - 2 * way
+        ref = ring_piece(axis, ((y if axis == 0 else z) - sign * (k - 1) + 8) % 8, 2 * j + p)
+        pltpu.make_async_remote_copy(
+            src_ref=ref, dst_ref=ref, send_sem=S["ring_s"].at[axis, k - 1],
+            recv_sem=S["ring_r"].at[axis, way, k - 1, j],
+            device_id=along("yz"[axis], sign + 8), device_id_type=MESH).start()
+
+    def ring_wait(axis, way, k, j):
+        whole(S["xg"].at[0, pl.ds(0, 2)], S["ring_s"].at[axis, 0], S["ring_r"].at[axis, way, k - 1, j]).wait_recv()
+
+    def ring_rest(k, j, carry):
+        for axis in (0, 1):
+            for way in (0, 1):
+                ring_wait(axis, way, k - 1, j)
+                for p in (0, 1):
+                    ring_send(axis, way, k, j, p)
+        return carry
+
+    def ring_last(j, carry):
+        for axis in (0, 1):
+            for way in (0, 1):
+                ring_wait(axis, way, 3, 2 * j + way)
+                for p in (0, 1):
+                    ring_send(axis, way, 4, 2 * j + way, p)
+        return carry
+
+    for e in range(8):
+        for axis in (0, 1):
+            if e:
+                (gx, gt)[axis][7 - offset(e)].wait_recv()
+            for way in (0, 1):
+                ring_send(axis, way, 1, e // 2, e % 2)
+    for axis in (0, 1):
+        for k in (1, 2, 3, 4):
+            ends.append(whole(
+                S["xg"].at[pl.ds(0, 2)] if k < 4 else S["xg"].at[0],
+                S["ring_s"].at[axis, k - 1], S["ring_r"].at[axis, 0, 0, 0]).wait_send)
     arrive(sta)
     S["stb"][d] = jnp.sum(S["sta"][...], axis=0)
-    stb = spread("stb", d, "ssb", "dp")
+    stb = spread("stb", d, 2, "dp")
     arrive(ggain)
-    load1.wait()
-    load2.wait()
+    for load in loads:
+        load()
+        ends.remove(load)
     total = jnp.zeros((8, H), f32)
     for i in range(8):
         rows = S["gg"][i]
         S["gb"][i] = turned(rows[0:1])[:F]
         total += jnp.dot(rows[:, :F].astype(bf16), S["w1"][F * i:F * (i + 1)], preferred_element_type=f32)
     S["u"][...] = total
-    ring_step(2)
+    lax.fori_loop(0, 4, functools.partial(ring_rest, 2), 0)
     arrive(stb)
     S["stc"][z] = jnp.sum(S["stb"][...], axis=0)
-    stc = spread("stc", z, "ssc", "z")
-    ring_step(3)
+    stc = spread("stc", z, 3, "z")
+    lax.fori_loop(0, 4, functools.partial(ring_rest, 3), 0)
     arrive(stc)
-    ring_step(4)
+    lax.fori_loop(0, 2, ring_last, 0)
     for axis in (0, 1):
         for way in (0, 1):
-            ring[axis, way, 3, 1 - way].wait_recv()
-            ring[axis, way, 4, way].wait_recv()
+            for j in (0, 1):
+                ring_wait(axis, way, 3, 2 * j + 1 - way)
+                ring_wait(axis, way, 4, 2 * j + way)
+    yield "ring"
 
     def scale_of(tile):
         mean = tile[0:1] / D
@@ -226,6 +285,8 @@
         act_part = jnp.dot(S["w2"][...], pair(S["tg"], i), preferred_element_type=f32)
         S["part"][0, :, :, :, lanes] = pre_part.reshape(4, 2, Q, 256)
         S["part"][1, :, :, :, lanes] = act_part.reshape(4, 2, Q, 256)
+
+    yield "products"
 
     pairs = []
     for i in (1, 2, 3, 0):
@@ -251,6 +312,7 @@
     pre_grad = (act_grad * slope).astype(bf16)
     S["comb"][d, 0] = value.astype(bf16)
     S["comb"][d, 1] = pre_grad
+    yield "dpsum"
     second = jnp.sum(pre_grad.astype(f32) * pre_act, axis=0, keepdims=True)
 
     hops = [
@@ -264,6 +326,8 @@
         pairs.append(go(
             S["comb"].at[slot], S["comb"].at[slot], "ac", (i,), at(2 * chip + 1 - core, z, y)))
     arrive(pairs)
+
+    yield "dpgather"
 
     for i in range(4):
         lanes = slice(256 * i, 256 * (i + 1))
@@ -311,26 +375,27 @@
         lanes = slice(128 * i, 128 * (i + 1))
         S["s2p"][i, 0:1] = first[0:1, lanes]
         S["s2p"][i, 1:2] = second[:, lanes]
-    s2a = [
-        go(S["s2p"].at[(d + i) % 8], S["s2r"].at[d], "s2a", (i - 1,), along("dp", i)) for i in range(1, 8)]
+    s2a = spread("s2r", d, 4, "dp", lambda i: S["s2p"].at[(d + i) % 8])
     S["s2r"][d] = S["s2p"][d]
     rs_step(2)
     nt_all = jnp.concatenate([S["nt"][i].reshape(K, 128) for i in range(8)], axis=1)
     S["w1g"][...] = lax.dot_general(nt_all, pg, (((1,), (1,)), ((), ())), preferred_element_type=f32)
     store1 = pltpu.make_async_copy(S["w1g"], w1g_hbm, S["loc"].at[2])
     store1.start()
+    ends.append(store1.wait)
     arrive(s2a)
     S["s2y"][y] = jnp.sum(S["s2r"][...], axis=0)
-    s2b = spread("s2y", y, "s2b", "y")
+    s2b = spread("s2y", y, 5, "y")
     rs_step(3)
     tg_all = jnp.concatenate([S["tg"][i].reshape(K, 128) for i in range(8)], axis=1)
     S["w2g"][...] = lax.dot_general(
         S["comb"][:, 0].reshape(H, 1024), tg_all, (((1,), (1,)), ((), ())), preferred_element_type=f32)
     store2 = pltpu.make_async_copy(S["w2g"], w2g_hbm, S["loc"].at[3])
     store2.start()
+    ends.append(store2.wait)
     arrive(s2b)
     S["s2z"][z] = jnp.sum(S["s2y"][...], axis=0)
-    s2c = spread("s2z", z, "s2c", "z")
+    s2c = spread("s2z", z, 6, "z")
     rs_step(4)
     arrive(s2c)
     for axis in (0, 1):
@@ -341,7 +406,8 @@
                 val = rs_add(axis, way, 4, sub, val)
             S["fs"][axis, half] = val.astype(bf16)
 
-    fins = []
+    yield "rings"
+
     for axis in (0, 1):
         for i in range(8):
             if axis == 0:
@@ -352,7 +418,10 @@
                 step = (y + i) % 8
                 dev, slot = at(z, d, step), y
                 clear = jnp.logical_or(off_diag, step != y)
-            copy = remote(S["fs"].at[axis, step], S["fr"].at[axis, slot], "fin", (axis, i), dev, (axis, slot))
+            copy = pltpu.make_async_remote_copy(
+                src_ref=S["fs"].at[axis, step], dst_ref=S["fr"].at[axis, slot],
+                send_sem=S["fin_s"].at[axis, int(i > 0)], recv_sem=S["fin_r"].at[axis],
+                device_id=dev, device_id_type=MESH)
             if i:
                 copy.start()
             else:
@@ -363,43 +432,23 @@
                 @pl.when(jnp.logical_not(clear))
                 def _():
                     pltpu.make_async_copy(
-                        S["fs"].at[axis, step], S["fr"].at[axis, slot], S["fin"].at[1, axis, slot]).start()
-            fins.append((copy, i, clear))
+                        S["fs"].at[axis, step], S["fr"].at[axis, slot], S["fin_r"].at[axis]).start()
+                ends.append(functools.partial(when_wait, clear, copy))
+        ends.append(whole(S["fs"].at[axis, pl.ds(0, 7)], S["fin_s"].at[axis, 1], S["fin_r"].at[axis]).wait_send)
     gcol = turned(S["gown"][0:1])[:F]
     mean, inv = scale_of(S["stc"][d])
-    cen = (S["own"][0].astype(f32) - mean) * inv
+    cen = (x_ref[...].astype(f32) - mean) * inv
     tile = jnp.sum(S["s2z"][...], axis=0)
-    base = S["own"][1].astype(f32) - inv * (tile[0:1] / D + cen * (tile[1:2] / D))
+    base = t_ref[...].astype(f32) - inv * (tile[0:1] / D + cen * (tile[1:2] / D))
     for axis in (0, 1):
-        for slot in range(8):
-            remote(S["fs"].at[axis, slot], S["fr"].at[axis, slot], "fin", (axis, slot), at(z, d, y)).wait_recv()
-        S["pad"][0, HALF * axis:HALF * (axis + 1)] = jnp.sum(S["fr"][axis].astype(f32), axis=0)
-    grad = S["pad"][0, :F]
-    S["pad"][1, :F] = grad * cen
-    S["ge"][d] = jnp.broadcast_to(jnp.sum(S["pad"][1].T, axis=0, keepdims=True), (8, 128))
-    ge = spread("ge", d, "gx", "dp")
-    S["pad"][0, :F] = base + inv * (grad * gcol)
-    ig_ref[...] = S["pad"][0].T[:, :F].astype(bf16)
+        whole(S["fr"].at[axis], S["fin_s"].at[axis, 1], S["fin_r"].at[axis]).wait_recv()
+    grad = jnp.concatenate([jnp.sum(S["fr"][axis].astype(f32), axis=0) for axis in (0, 1)], axis=0)
+    S["pad"][:F] = grad * cen
+    S["ge"][d] = jnp.broadcast_to(jnp.sum(S["pad"][...].T, axis=0, keepdims=True), (8, 128))
+    ge = spread("ge", d, 7, "dp")
+    ig_ref[...] = (base + inv * (grad * gcol)).astype(bf16)
     arrive(ge)
     gg_out[...] = jnp.sum(S["ge"][...], axis=0)
-
-    for copy in sends:
-        copy.wait_send()
-    for copy, i, clear in fins:
-        if i:
-            copy.wait_send()
-        else:
-            @pl.when(clear)
-            def _():
-                copy.wait_send()
-
-    @pl.when(off_diag)
-    def _():
-        for copy in perm:
-            copy.wait_send()
-
-    store1.wait()
-    store2.wait()
 
 
 def shards(inputs, gain, w_in, w_out, targets):
@@ -409,17 +458,17 @@
     input_grad, gain_grad, w_in_grad, w_out_grad = pl.pallas_call(
         kernel,
         out_shape=(
-            jax.ShapeDtypeStruct((128, F), bf16), jax.ShapeDtypeStruct((8, 128), f32),
+            jax.ShapeDtypeStruct((F, 128), bf16), jax.ShapeDtypeStruct((8, 128), f32),
             jax.ShapeDtypeStruct((K, H), f32), jax.ShapeDtypeStruct((H, K), f32)),
         in_specs=[vmem, vmem, vmem, hbm, hbm],
         out_specs=(vmem, vmem, hbm, hbm),
         scratch_shapes=scratch,
         compiler_params=pltpu.CompilerParams(
-            collective_id=0, has_side_effects=True, vmem_limit_bytes=48 * 1024 * 1024),
+            collective_id=0, has_side_effects=True, vmem_limit_bytes=60 * 1024 * 1024),
         cost_estimate=pl.CostEstimate(flops=2 * 10 ** 9, bytes_accessed=4 * 10 ** 6, transcendentals=10 ** 5),
         name="backward",
-    )(inputs, targets, gain.reshape(1, F), w_in, w_out)
-    return input_grad, gain_grad[0, :F], w_in_grad, w_out_grad
+    )(inputs.T, targets.T, gain.reshape(1, F), w_in, w_out)
+    return input_grad.T, gain_grad[0, :F], w_in_grad, w_out_grad
 
 
 def solution(mesh):

time: 117 us -> 112 us (0.957)
  Pallas kernels: 110 us -> 105 us
    pallas_call x1, Pallas kernels: 110 us -> 105 us  [shards(): pl.pallas_call(kernel, out_shape=(jax.ShapeDtypeStruct((F, 128), bf16), j...]
    unnamed x13 -> x5, local copies, waits for them, and re-layouts: 5.95 us -> 4.36 us
where the time goes in v2:
time: 112 us
  Pallas kernels  105 us (94%)
  local copies, waits for them, and re-layouts  5.55 us (5%)
    pallas_call x1, Pallas kernels, shards(): pl.pallas_call(kernel, out_shape=(jax.ShapeDtypeStruct((F, 128), bf16), j...  105 us
    unnamed x5, local copies, waits for them, and re-layouts  4.36 us

profile of v2, /device:TPU:1, one launch (start us, length us, event | category | flops | bytes accessed | tf_op | source)
XLA Modules:
  0.0 111.6 jit_solution(382808533141913156)
XLA Ops:
  0.6 105.4 %backward.1 = (bf16[96,128]{1,0:T(8,128)(2,1)}, f32[8,128]{1,0:T(8,128)}, f32[768,256]{1,0:T(8,128)}, f32[256,768]{1,0:T(8,128)}) custom-call(bf16[96,128]{1,0:T(8,128)(2,1)} %bitcast.7, bf16[96,128]{1,0:T(8,128)(2,1)} %bitcast.8, bf16[1,96]{1,0:T(2,128)(2,1)} %bitcast.9, bf16[768,256]{1,0:T(8,128)(2,1)} %refs_3_.1, bf16[256,768]{1,0:T(8,128)(2,1)} %refs_4_.1), custom_call_target="tpu_custom_call" | custom-call | flops 2000000000 | bytes 4000000 | tf_op jit(solution)/shard_map/backward/pallas_call | solution.py:458
  106.0 1.2 %slice_bitcast_fusion = f32[96]{0:T(128)} fusion(f32[8,128]{1,0:T(8,128)} %get-tuple-element.9), kind=kLoop, calls=%fused_computation | loop fusion | bytes 768 | tf_op jit(solution)/shard_map/squeeze | solution.py:471
  107.2 1.3 %copy.12 = bf16[128,96]{0,1:T(8,128)(2,1)} copy(bf16[128,96]{0,1:T(8,128)(2,1)} %bitcast.6) | data formatting | bytes 49152
  108.5 0.0 copy-start
  108.5 2.1 %copy.13 = f32[768,256]{1,0:T(8,128)} copy(f32[768,256]{1,0:T(8,128)} %get-tuple-element.18) | data formatting | bytes 1572864
  110.7 0.0 copy-done
  110.7 0.9 copy.14
Async XLA Ops:
  108.5 2.1 %copy-start = (f32[256,768]{1,0:T(8,128)S(1)}, f32[256,768]{1,0:T(8,128)}, u32[]{:S(2)}) copy-start(f32[256,768]{1,0:T(8,128)} %get-tuple-element.19) | copy-start | bytes 2359300

commit v3 on v2

--- a/solution.py
+++ b/solution.py
@@ -40,18 +40,17 @@
     xg=((8, 8, F, 128), bf16), tg=((8, 8, F, 128), bf16), nt=((8, 8, F, 128), bf16),
     gg=((8, 8, 128), f32), gb=((8, F, 128), f32),
     sta=((8, 8, 128), f32), stb=((8, 8, 128), f32), stc=((8, 8, 128), f32),
-    part=((2, 4, 2, Q, 1024), f32), cs=((4, 2, Q, 1024), bf16), cr=((4, 2, Q, 1024), bf16),
-    xs=((3, 2, Q, 1024), bf16), xr=((3, 2, Q, 1024), bf16),
-    pre=((2, Q, 1024), f32), comb=((8, 2, Q, 1024), bf16),
+    part=((2, 2, 4, 2, Q, 512), f32), cs=((2, 4, 2, Q, 512), bf16), cr=((2, 4, 2, Q, 512), bf16),
+    xs=((2, 3, 2, Q, 512), bf16), xr=((2, 3, 2, Q, 512), bf16), comb=((2, 8, 2, Q, 512), bf16),
     u=((8, H), f32), s2p=((8, 8, 128), f32), s2r=((8, 8, 128), f32),
     s2y=((8, 8, 128), f32), s2z=((8, 8, 128), f32),
     ng=((8, 8, F, 128), f32), ra=((2, 2, 4, 8, HALF, 128), bf16), sa=((2, 2, 4, 8, HALF, 128), bf16),
-    fs=((2, 8, HALF, 128), bf16), fr=((2, 8, HALF, 128), bf16),
-    w1g=((K, H), f32), w2g=((H, K), f32), ge=((8, 8, 128), f32),
+    fs=((8, 2, HALF, 128), bf16), ft=((8, 2, HALF, 128), bf16), fr=((2, 8, HALF, 128), bf16),
+    w1g=((K, H), f32), w2g=((H, K), f32), gs=((8, 8, 128), f32), gr=((2, 8, 8, 128), f32),
 )
 SEMS = dict(
     loc=(4,), perm=(2, 3), sx=(2, 7), stg=(2, 7), small=(2, 10), ring_s=(2, 4), ring_r=(2, 2, 4, 4),
-    core=(2, 4), xx=(2, 3), ax=(2, 3), ac=(2, 4), rs=(2, 2, 2, 4, 2), fin_s=(2, 2), fin_r=(2,),
+    core=(2, 2, 4), xx=(2, 2, 3), ax=(2, 2, 3), ac=(2, 2, 4), rs=(2, 2, 2, 4, 2), fin=(2, 6),
 )
 
 
@@ -278,106 +277,122 @@
         return jnp.concatenate(
             [ref[2 * i].reshape(K, 128), ref[2 * i + 1].reshape(K, 128)], axis=1)
 
-    for i in range(4):
-        lanes = slice(256 * i, 256 * (i + 1))
-        pre_part = lax.dot_general(
-            S["w1"][...], pair(S["nt"], i), (((0,), (0,)), ((), ())), preferred_element_type=f32)
-        act_part = jnp.dot(S["w2"][...], pair(S["tg"], i), preferred_element_type=f32)
-        S["part"][0, :, :, :, lanes] = pre_part.reshape(4, 2, Q, 256)
-        S["part"][1, :, :, :, lanes] = act_part.reshape(4, 2, Q, 256)
-
+    def products(h):
+        for i in (2 * h, 2 * h + 1):
+            lanes = slice(256 * (i % 2), 256 * (i % 2 + 1))
+            pre_part = lax.dot_general(
+                S["w1"][...], pair(S["nt"], i), (((0,), (0,)), ((), ())), preferred_element_type=f32)
+            act_part = jnp.dot(S["w2"][...], pair(S["tg"], i), preferred_element_type=f32)
+            S["part"][h, 0, :, :, :, lanes] = pre_part.reshape(4, 2, Q, 256)
+            S["part"][h, 1, :, :, :, lanes] = act_part.reshape(4, 2, Q, 256)
+        pairs = {}
+        for i in (1, 2, 3, 0):
+            to = (chip + i) % 4
+            for arr in range(2):
+                S["cs"][h, to, arr] = S["part"][h, arr, to, 1 - core].astype(bf16)
+            pairs[i] = go(S["cs"].at[h, to], S["cr"].at[h, to], "core", (h, i), at(2 * chip + 1 - core, z, y))
+        return pairs
+
+    def chip_sum(h, pairs):
+        hops = []
+        for i in (1, 2, 3):
+            to = (chip + i) % 4
+            pairs[i].wait_recv()
+            for arr in range(2):
+                S["xs"][h, i - 1, arr] = (
+                    S["part"][h, arr, to, core] + S["cr"][h, to, arr].astype(f32)).astype(bf16)
+            hops.append(go(S["xs"].at[h, i - 1], S["xr"].at[h, i - 1], "xx", (h, i - 1), at(2 * to + core, z, y)))
+        return hops
+
+    def activate(h, pairs, hops):
+        pairs[0].wait_recv()
+        arrive(hops)
+        pre_act, act_grad = (
+            S["part"][h, arr, chip, core] + S["cr"][h, chip, arr].astype(f32)
+            + sum(S["xr"][h, i, arr].astype(f32) for i in range(3)) for arr in range(2))
+        value, slope = gelu_parts(pre_act)
+        pre_grad = (act_grad * slope).astype(bf16)
+        S["comb"][h, d, 0] = value.astype(bf16)
+        S["comb"][h, d, 1] = pre_grad
+        hops = {
+            i: go(S["comb"].at[h, d], S["comb"].at[h, d], "ax", (h, i - 1), at(2 * ((chip + i) % 4) + core, z, y))
+            for i in (1, 2, 3)}
+        second = jnp.sum(pre_grad.astype(f32) * pre_act, axis=0, keepdims=True)
+        for i in range(4):
+            S["s2p"][4 * h + i] = jnp.zeros((8, 128), f32)
+            S["s2p"][4 * h + i, 1:2] = second[:, 128 * i:128 * (i + 1)]
+        return hops
+
+    def pass_on(h, hops):
+        pairs = []
+        for i in (0, 3, 1, 2):
+            slot = 2 * ((chip - i + 4) % 4) + core
+            if i:
+                hops[i].wait_recv()
+            ref = S["comb"].at[h, slot]
+            pairs.append(go(ref, ref, "ac", (h, i), at(2 * chip + 1 - core, z, y)))
+        return pairs
+
+    both = (0, 1)
+    pairs = [products(h) for h in both]
     yield "products"
-
-    pairs = []
-    for i in (1, 2, 3, 0):
-        to = (chip + i) % 4
-        for arr in range(2):
-            S["cs"][to, arr] = S["part"][arr, to, 1 - core].astype(bf16)
-        pairs.append(go(S["cs"].at[to], S["cr"].at[to], "core", (i,), at(2 * chip + 1 - core, z, y)))
-    hops = []
-    for i in (1, 2, 3):
-        to = (chip + i) % 4
-        pairs[i - 1].wait_recv()
-        for arr in range(2):
-            S["xs"][i - 1, arr] = (S["part"][arr, to, core] + S["cr"][to, arr].astype(f32)).astype(bf16)
-        hops.append(go(S["xs"].at[i - 1], S["xr"].at[i - 1], "xx", (i - 1,), at(2 * to + core, z, y)))
-    pairs[3].wait_recv()
-    for arr in range(2):
-        S["pre"][arr] = S["part"][arr, chip, core] + S["cr"][chip, arr].astype(f32)
-    for i in range(3):
-        hops[i].wait_recv()
-    pre_act = S["pre"][0] + sum(S["xr"][i, 0].astype(f32) for i in range(3))
-    act_grad = S["pre"][1] + sum(S["xr"][i, 1].astype(f32) for i in range(3))
-    value, slope = gelu_parts(pre_act)
-    pre_grad = (act_grad * slope).astype(bf16)
-    S["comb"][d, 0] = value.astype(bf16)
-    S["comb"][d, 1] = pre_grad
+    hops = [chip_sum(h, pairs[h]) for h in both]
+    hops = [activate(h, pairs[h], hops[h]) for h in both]
     yield "dpsum"
-    second = jnp.sum(pre_grad.astype(f32) * pre_act, axis=0, keepdims=True)
-
-    hops = [
-        go(S["comb"].at[d], S["comb"].at[d], "ax", (i - 1,), at(2 * ((chip + i) % 4) + core, z, y))
-        for i in (1, 2, 3)]
-    pairs = []
-    for i in (0, 3, 2, 1):
-        slot = 2 * ((chip + i) % 4) + core
-        if i:
-            hops[3 - i].wait_recv()
-        pairs.append(go(
-            S["comb"].at[slot], S["comb"].at[slot], "ac", (i,), at(2 * chip + 1 - core, z, y)))
-    arrive(pairs)
-
+    pairs = [pass_on(h, hops[h]) for h in both]
+
+    def norm_products(h):
+        arrive(pairs[h])
+        for i in (2 * h, 2 * h + 1):
+            lanes = slice(256 * (i % 2), 256 * (i % 2 + 1))
+            out = jnp.dot(
+                S["w1"][...], S["comb"][h, :, 1, :, lanes].reshape(H, 256), preferred_element_type=f32)
+            S["ng"][2 * i] = out[:, :128].reshape(8, F, 128)
+            S["ng"][2 * i + 1] = out[:, 128:].reshape(8, F, 128)
+
+    rs = {}
+
+    def rs_block(axis, dest, h):
+        return S["ng"][pl.ds(4 * h, 4), dest, HALF * axis:HALF * (axis + 1)]
+
+    def rs_add(axis, way, k, h, val):
+        if (axis, way, k, h) in rs:
+            rs[axis, way, k, h].wait_recv()
+            val = val + S["ra"][axis, way, k - 1, pl.ds(4 * h, 4)].astype(f32)
+        return val
+
+    def rs_round(r, h):
+        for axis in both:
+            for way in both:
+                k = r + 1 if h == way else r + 2
+                if k > 4:
+                    continue
+                sign = 1 - 2 * way
+                me = y if axis == 0 else z
+                val = rs_block(axis, (me + sign * (5 - k) + 8) % 8, h)
+                val = rs_add(axis, way, k - 1, h, val)
+                half = pl.ds(4 * h, 4)
+                S["sa"][axis, way, k - 1, half] = val.astype(bf16)
+                rs[axis, way, k, h] = go(
+                    S["sa"].at[axis, way, k - 1, half], S["ra"].at[axis, way, k - 1, half],
+                    "rs", (axis, way, k - 1, h), along("yz"[axis], sign + 8))
+
+    norm_products(0)
+    rs_round(0, 0)
+    norm_products(1)
     yield "dpgather"
-
-    for i in range(4):
-        lanes = slice(256 * i, 256 * (i + 1))
-        out = jnp.dot(S["w1"][...], S["comb"][:, 1, :, lanes].reshape(H, 256), preferred_element_type=f32)
-        S["ng"][2 * i] = out[:, :128].reshape(8, F, 128)
-        S["ng"][2 * i + 1] = out[:, 128:].reshape(8, F, 128)
-
-    rs = {}
-
-    def rs_block(axis, dest, sub):
-        half = pl.ds(4 * sub, 4)
-        if axis == 0:
-            return S["ng"][half, dest, 0:HALF]
-        return S["ng"][dest, half, HALF:F]
-
-    def rs_add(axis, way, k, sub, val):
-        if (axis, way, k, sub) in rs:
-            rs[axis, way, k, sub].wait_recv()
-            val = val + S["ra"][axis, way, k - 1, pl.ds(4 * sub, 4)].astype(f32)
-        return val
-
-    def rs_step(k):
-        for sub in (0, 1):
-            for axis in (0, 1):
-                for way in (0, 1):
-                    if k == 1 and sub != way:
-                        continue
-                    sign = 1 - 2 * way
-                    me = y if axis == 0 else z
-                    val = rs_block(axis, (me + sign * (5 - k) + 8) % 8, sub)
-                    val = rs_add(axis, way, k - 1, sub, val)
-                    half = pl.ds(4 * sub, 4)
-                    S["sa"][axis, way, k - 1, half] = val.astype(bf16)
-                    rs[axis, way, k, sub] = go(
-                        S["sa"].at[axis, way, k - 1, half], S["ra"].at[axis, way, k - 1, half],
-                        "rs", (axis, way, k - 1, sub), along("yz"[axis], sign + 8))
-
-    rs_step(1)
-    pg = S["comb"][:, 1].reshape(H, 1024)
+    rs_round(0, 1)
+    pg, act = (
+        jnp.concatenate([S["comb"][h, :, arr].reshape(H, 512) for h in both], axis=1) for arr in (1, 0))
     high = S["u"][...].astype(bf16)
     low = (S["u"][...] - high.astype(f32)).astype(bf16)
     first = jnp.dot(high, pg, preferred_element_type=f32) + jnp.dot(low, pg, preferred_element_type=f32)
-    S["s2p"][...] = jnp.zeros_like(S["s2p"])
     for i in range(8):
-        lanes = slice(128 * i, 128 * (i + 1))
-        S["s2p"][i, 0:1] = first[0:1, lanes]
-        S["s2p"][i, 1:2] = second[:, lanes]
+        S["s2p"][i, 0:1] = first[0:1, 128 * i:128 * (i + 1)]
     s2a = spread("s2r", d, 4, "dp", lambda i: S["s2p"].at[(d + i) % 8])
     S["s2r"][d] = S["s2p"][d]
-    rs_step(2)
+    rs_round(1, 0)
+    rs_round(1, 1)
     nt_all = jnp.concatenate([S["nt"][i].reshape(K, 128) for i in range(8)], axis=1)
     S["w1g"][...] = lax.dot_general(nt_all, pg, (((1,), (1,)), ((), ())), preferred_element_type=f32)
     store1 = pltpu.make_async_copy(S["w1g"], w1g_hbm, S["loc"].at[2])
@@ -386,69 +401,82 @@
     arrive(s2a)
     S["s2y"][y] = jnp.sum(S["s2r"][...], axis=0)
     s2b = spread("s2y", y, 5, "y")
-    rs_step(3)
+    rs_round(2, 0)
+    rs_round(2, 1)
     tg_all = jnp.concatenate([S["tg"][i].reshape(K, 128) for i in range(8)], axis=1)
-    S["w2g"][...] = lax.dot_general(
-        S["comb"][:, 0].reshape(H, 1024), tg_all, (((1,), (1,)), ((), ())), preferred_element_type=f32)
+    S["w2g"][...] = lax.dot_general(act, tg_all, (((1,), (1,)), ((), ())), preferred_element_type=f32)
     store2 = pltpu.make_async_copy(S["w2g"], w2g_hbm, S["loc"].at[3])
     store2.start()
     ends.append(store2.wait)
     arrive(s2b)
     S["s2z"][z] = jnp.sum(S["s2y"][...], axis=0)
     s2c = spread("s2z", z, 6, "z")
-    rs_step(4)
+    rs_round(3, 0)
+    rs_round(3, 1)
     arrive(s2c)
-    for axis in (0, 1):
-        for sub in (0, 1):
-            half = pl.ds(4 * sub, 4)
-            val = rs_block(axis, y if axis == 0 else z, sub)
-            for way in (0, 1):
-                val = rs_add(axis, way, 4, sub, val)
-            S["fs"][axis, half] = val.astype(bf16)
-
+    for axis in both:
+        for h in both:
+            val = rs_block(axis, y if axis == 0 else z, h)
+            for way in both:
+                val = rs_add(axis, way, 4, h, val)
+            S["ng"][pl.ds(4 * h, 4), y if axis == 0 else z, HALF * axis:HALF * (axis + 1)] = val
+            S["fs"][pl.ds(4 * h, 4), axis] = val.astype(bf16)
     yield "rings"
 
-    for axis in (0, 1):
+    S["ft"][d] = S["fs"][d]
+    blocks = spread("ft", d, 7, "dp", lambda i: S["fs"].at[(d + i) % 8])
+    for axis, piece in ((0, y), (1, z)):
+        rows = slice(HALF * axis, HALF * (axis + 1))
+        total = jnp.zeros((HALF, 128), f32)
         for i in range(8):
-            if axis == 0:
-                step = (d + i) % 8
-                dev, slot = at(step, d, y), z
-                clear = jnp.logical_or(off_diag, step != d)
+            mean, inv = scale_of(S["stc"][i])
+            total += S["ng"][i, piece, rows] * ((S["xg"][i, piece, rows].astype(f32) - mean) * inv)
+        S["pad"][rows] = total
+    S["gs"][d] = jnp.broadcast_to(jnp.sum(S["pad"][...].T, axis=0, keepdims=True), (8, 128))
+    gains = spread("gs", d, 8, "dp")
+
+    def deliver(number, axis, source, into):
+        for i in range(8):
+            block = (z + i) % 8
+            dev, slot = (at(d, block, y), z) if axis == 0 else (at(d, block, z), y)
+            def send():
+                return pltpu.make_async_remote_copy(
+                    src_ref=source(block), dst_ref=into.at[axis, slot],
+                    send_sem=S["fin"].at[0, number if i else 4 + number // 2], recv_sem=S["fin"].at[1, number],
+                    device_id=dev, device_id_type=MESH)
+
+            def stay():
+                pltpu.make_async_copy(source(block), into.at[axis, slot], S["fin"].at[1, number]).start()
+
+            if i:
+                send().start()
+            elif axis == 0:
+                stay()
             else:
-                step = (y + i) % 8
-                dev, slot = at(z, d, step), y
-                clear = jnp.logical_or(off_diag, step != y)
-            copy = pltpu.make_async_remote_copy(
-                src_ref=S["fs"].at[axis, step], dst_ref=S["fr"].at[axis, slot],
-                send_sem=S["fin_s"].at[axis, int(i > 0)], recv_sem=S["fin_r"].at[axis],
-                device_id=dev, device_id_type=MESH)
-            if i:
-                copy.start()
-            else:
-                @pl.when(clear)
-                def _():
-                    copy.start()
-
-                @pl.when(jnp.logical_not(clear))
-                def _():
-                    pltpu.make_async_copy(
-                        S["fs"].at[axis, step], S["fr"].at[axis, slot], S["fin_r"].at[axis]).start()
-                ends.append(functools.partial(when_wait, clear, copy))
-        ends.append(whole(S["fs"].at[axis, pl.ds(0, 7)], S["fin_s"].at[axis, 1], S["fin_r"].at[axis]).wait_send)
+                pl.when(y != z)(lambda: send().start())
+                pl.when(y == z)(stay)
+                ends.append(functools.partial(when_wait, y != z, send()))
+        ends.append(whole(into.at[axis, pl.ds(0, 7)], S["fin"].at[0, number], S["fin"].at[1, number]).wait_send)
+
+    arrive(blocks)
+    for axis in both:
+        deliver(axis, axis, lambda block: S["ft"].at[block, axis], S["fr"])
+    arrive(gains)
+    for axis in both:
+        deliver(2 + axis, axis, lambda block: S["gs"].at[block], S["gr"])
     gcol = turned(S["gown"][0:1])[:F]
     mean, inv = scale_of(S["stc"][d])
     cen = (x_ref[...].astype(f32) - mean) * inv
     tile = jnp.sum(S["s2z"][...], axis=0)
     base = t_ref[...].astype(f32) - inv * (tile[0:1] / D + cen * (tile[1:2] / D))
-    for axis in (0, 1):
-        whole(S["fr"].at[axis], S["fin_s"].at[axis, 1], S["fin_r"].at[axis]).wait_recv()
-    grad = jnp.concatenate([jnp.sum(S["fr"][axis].astype(f32), axis=0) for axis in (0, 1)], axis=0)
-    S["pad"][:F] = grad * cen
-    S["ge"][d] = jnp.broadcast_to(jnp.sum(S["pad"][...].T, axis=0, keepdims=True), (8, 128))
-    ge = spread("ge", d, 7, "dp")
+    for axis in both:
+        whole(S["fr"].at[axis], S["fin"].at[0, axis], S["fin"].at[1, axis]).wait_recv()
+    grad = jnp.concatenate([jnp.sum(S["fr"][axis].astype(f32), axis=0) for axis in both], axis=0)
     ig_ref[...] = (base + inv * (grad * gcol)).astype(bf16)
-    arrive(ge)
-    gg_out[...] = jnp.sum(S["ge"][...], axis=0)
+    for axis in both:
+        whole(S["gr"].at[axis], S["fin"].at[0, 2 + axis], S["fin"].at[1, 2 + axis]).wait_recv()
+    lane = lax.broadcasted_iota(jnp.int32, (8, 128), 1)
+    gg_out[...] = jnp.where(lane < HALF, jnp.sum(S["gr"][0], axis=0), jnp.sum(S["gr"][1], axis=0))
 
 
 def shards(inputs, gain, w_in, w_out, targets):

time: 112 us -> 109 us (0.973); the launches traced: 112 us -> 107 us
  Pallas kernels: 105 us -> 101 us
    pallas_call x1, Pallas kernels: 105 us -> 101 us  [shards(): pl.pallas_call(kernel, out_shape=(jax.ShapeDtypeStruct((F, 128), bf16), j...]
where the time goes in v3:
time: 109 us; the launch traced here: 107 us
  Pallas kernels  101 us (93%)
  local copies, waits for them, and re-layouts  5.55 us (5%)
    pallas_call x1, Pallas kernels, shards(): pl.pallas_call(kernel, out_shape=(jax.ShapeDtypeStruct((F, 128), bf16), j...  101 us
    unnamed x5, local copies, waits for them, and re-layouts  4.36 us

profile of v3, /device:TPU:1, one launch (start us, length us, event | category | flops | bytes accessed | tf_op | source)
XLA Modules:
  0.0 107.2 jit_solution(395996150042138165)
XLA Ops:
  0.6 101.0 %backward.1 = (bf16[96,128]{1,0:T(8,128)(2,1)}, f32[8,128]{1,0:T(8,128)}, f32[768,256]{1,0:T(8,128)}, f32[256,768]{1,0:T(8,128)}) custom-call(bf16[96,128]{1,0:T(8,128)(2,1)} %bitcast.7, bf16[96,128]{1,0:T(8,128)(2,1)} %bitcast.8, bf16[1,96]{1,0:T(2,128)(2,1)} %bitcast.9, bf16[768,256]{1,0:T(8,128)(2,1)} %refs_3_.1, bf16[256,768]{1,0:T(8,128)(2,1)} %refs_4_.1), custom_call_target="tpu_custom_call" | custom-call | flops 2000000000 | bytes 4000000 | tf_op jit(solution)/shard_map/backward/pallas_call | solution.py:486
  101.6 1.2 %slice_bitcast_fusion = f32[96]{0:T(128)} fusion(f32[8,128]{1,0:T(8,128)} %get-tuple-element.9), kind=kLoop, calls=%fused_computation | loop fusion | bytes 768 | tf_op jit(solution)/shard_map/squeeze | solution.py:499
  102.8 1.3 %copy.12 = bf16[128,96]{0,1:T(8,128)(2,1)} copy(bf16[128,96]{0,1:T(8,128)(2,1)} %bitcast.6) | data formatting | bytes 49152
  104.2 0.0 copy-start
  104.2 2.1 %copy.13 = f32[768,256]{1,0:T(8,128)} copy(f32[768,256]{1,0:T(8,128)} %get-tuple-element.18) | data formatting | bytes 1572864
  106.3 0.0 copy-done
  106.3 0.9 copy.14
Async XLA Ops:
  104.2 2.1 %copy-start = (f32[256,768]{1,0:T(8,128)S(1)}, f32[256,768]{1,0:T(8,128)}, u32[]{:S(2)}) copy-start(f32[256,768]{1,0:T(8,128)} %get-tuple-element.19) | copy-start | bytes 2359300

commit v4 on v3

--- a/solution.py
+++ b/solution.py
@@ -22,12 +22,6 @@
     cumul = 0.5 * (1.0 + lax.erf(values * 0.7071067811865476))
     slope = cumul + values * jnp.exp(-0.5 * values * values) * 0.3989422804014327
     return values * cumul, slope
-
-
-def when_wait(cond, copy):
-    @pl.when(cond)
-    def _():
-        copy.wait_send()
 
 
 def turned(rows):
@@ -45,23 +39,19 @@
     u=((8, H), f32), s2p=((8, 8, 128), f32), s2r=((8, 8, 128), f32),
     s2y=((8, 8, 128), f32), s2z=((8, 8, 128), f32),
     ng=((8, 8, F, 128), f32), ra=((2, 2, 4, 8, HALF, 128), bf16), sa=((2, 2, 4, 8, HALF, 128), bf16),
-    fs=((8, 2, HALF, 128), bf16), ft=((8, 2, HALF, 128), bf16), fr=((2, 8, HALF, 128), bf16),
-    w1g=((K, H), f32), w2g=((H, K), f32), gs=((8, 8, 128), f32), gr=((2, 8, 8, 128), f32),
+    fs=((8, 2, HALF, 128), bf16), ft=((8, 2, HALF, 128), bf16), fr=((8, 2, HALF, 128), bf16),
+    w1g=((K, H), f32), w2g=((H, K), f32), gs=((8, 8, 128), f32), gr=((8, 8, 128), f32),
 )
 SEMS = dict(
-    loc=(4,), perm=(2, 3), sx=(2, 7), stg=(2, 7), small=(2, 10), ring_s=(2, 4), ring_r=(2, 2, 4, 4),
-    core=(2, 2, 4), xx=(2, 2, 3), ax=(2, 2, 3), ac=(2, 2, 4), rs=(2, 2, 2, 4, 2), fin=(2, 6),
+    loc=(4,), perm=(2, 3), sx=(2, 7), stg=(2, 7), small=(2, 11), ring_s=(2, 4), ring_r=(2, 2, 4, 4),
+    core=(2, 2, 4), xx=(2, 2, 3), ax=(2, 2, 3), ac=(2, 2, 4), rs=(2, 2, 2, 4, 2),
 )
-
-
-LAST = None
 
 
 def kernel(*refs):
     ends = []
-    for name in phases(ends, *refs):
-        if name == LAST:
-            break
+    for _ in phases(ends, *refs):
+        pass
     for end in ends:
         end()
 
@@ -144,9 +134,7 @@
     def _():
         pl.semaphore_wait(barrier, 21)
 
-    if LAST == "barrier":
-        return
-
+    yield "barrier"
     perm = [
         (x_ref, S["xg"].at[d, y]),
         (t_ref, S["tg"].at[d, y]),
@@ -234,6 +222,7 @@
             ends.append(whole(
                 S["xg"].at[pl.ds(0, 2)] if k < 4 else S["xg"].at[0],
                 S["ring_s"].at[axis, k - 1], S["ring_r"].at[axis, 0, 0, 0]).wait_send)
+    yield "ring1"
     arrive(sta)
     S["stb"][d] = jnp.sum(S["sta"][...], axis=0)
     stb = spread("stb", d, 2, "dp")
@@ -248,10 +237,12 @@
         total += jnp.dot(rows[:, :F].astype(bf16), S["w1"][F * i:F * (i + 1)], preferred_element_type=f32)
     S["u"][...] = total
     lax.fori_loop(0, 4, functools.partial(ring_rest, 2), 0)
+    yield "ring2"
     arrive(stb)
     S["stc"][z] = jnp.sum(S["stb"][...], axis=0)
     stc = spread("stc", z, 3, "z")
     lax.fori_loop(0, 4, functools.partial(ring_rest, 3), 0)
+    yield "ring3"
     arrive(stc)
     lax.fori_loop(0, 2, ring_last, 0)
     for axis in (0, 1):
@@ -337,6 +328,7 @@
     pairs = [products(h) for h in both]
     yield "products"
     hops = [chip_sum(h, pairs[h]) for h in both]
+    yield "chipsum"
     hops = [activate(h, pairs[h], hops[h]) for h in both]
     yield "dpsum"
     pairs = [pass_on(h, hops[h]) for h in both]
@@ -368,15 +360,15 @@
                 if k > 4:
                     continue
                 sign = 1 - 2 * way
-                me = y if axis == 0 else z
-                val = rs_block(axis, (me + sign * (5 - k) + 8) % 8, h)
+                val = rs_block(axis, (y + sign * (5 - k) + 8) % 8, h)
                 val = rs_add(axis, way, k - 1, h, val)
                 half = pl.ds(4 * h, 4)
                 S["sa"][axis, way, k - 1, half] = val.astype(bf16)
                 rs[axis, way, k, h] = go(
                     S["sa"].at[axis, way, k - 1, half], S["ra"].at[axis, way, k - 1, half],
-                    "rs", (axis, way, k - 1, h), along("yz"[axis], sign + 8))
-
+                    "rs", (axis, way, k - 1, h), along("y", sign + 8))
+
+    yield "passon"
     norm_products(0)
     rs_round(0, 0)
     norm_products(1)
@@ -393,90 +385,82 @@
     S["s2r"][d] = S["s2p"][d]
     rs_round(1, 0)
     rs_round(1, 1)
+    yield "round1"
     nt_all = jnp.concatenate([S["nt"][i].reshape(K, 128) for i in range(8)], axis=1)
     S["w1g"][...] = lax.dot_general(nt_all, pg, (((1,), (1,)), ((), ())), preferred_element_type=f32)
     store1 = pltpu.make_async_copy(S["w1g"], w1g_hbm, S["loc"].at[2])
     store1.start()
     ends.append(store1.wait)
+    yield "w1g"
     arrive(s2a)
     S["s2y"][y] = jnp.sum(S["s2r"][...], axis=0)
     s2b = spread("s2y", y, 5, "y")
     rs_round(2, 0)
     rs_round(2, 1)
+    yield "round2"
     tg_all = jnp.concatenate([S["tg"][i].reshape(K, 128) for i in range(8)], axis=1)
     S["w2g"][...] = lax.dot_general(act, tg_all, (((1,), (1,)), ((), ())), preferred_element_type=f32)
     store2 = pltpu.make_async_copy(S["w2g"], w2g_hbm, S["loc"].at[3])
     store2.start()
     ends.append(store2.wait)
+    yield "w2g"
     arrive(s2b)
     S["s2z"][z] = jnp.sum(S["s2y"][...], axis=0)
     s2c = spread("s2z", z, 6, "z")
     rs_round(3, 0)
     rs_round(3, 1)
+    yield "round3"
     arrive(s2c)
     for axis in both:
         for h in both:
-            val = rs_block(axis, y if axis == 0 else z, h)
+            val = rs_block(axis, y, h)
             for way in both:
                 val = rs_add(axis, way, 4, h, val)
-            S["ng"][pl.ds(4 * h, 4), y if axis == 0 else z, HALF * axis:HALF * (axis + 1)] = val
+            S["ng"][pl.ds(4 * h, 4), y, HALF * axis:HALF * (axis + 1)] = val
             S["fs"][pl.ds(4 * h, 4), axis] = val.astype(bf16)
     yield "rings"
 
     S["ft"][d] = S["fs"][d]
     blocks = spread("ft", d, 7, "dp", lambda i: S["fs"].at[(d + i) % 8])
-    for axis, piece in ((0, y), (1, z)):
-        rows = slice(HALF * axis, HALF * (axis + 1))
-        total = jnp.zeros((HALF, 128), f32)
-        for i in range(8):
-            mean, inv = scale_of(S["stc"][i])
-            total += S["ng"][i, piece, rows] * ((S["xg"][i, piece, rows].astype(f32) - mean) * inv)
-        S["pad"][rows] = total
+    total = jnp.zeros((F, 128), f32)
+    for i in range(8):
+        mean, inv = scale_of(S["stc"][i])
+        total += S["ng"][i, y] * ((S["xg"][i, y].astype(f32) - mean) * inv)
+    S["pad"][:F] = total
     S["gs"][d] = jnp.broadcast_to(jnp.sum(S["pad"][...].T, axis=0, keepdims=True), (8, 128))
     gains = spread("gs", d, 8, "dp")
 
-    def deliver(number, axis, source, into):
-        for i in range(8):
-            block = (z + i) % 8
-            dev, slot = (at(d, block, y), z) if axis == 0 else (at(d, block, z), y)
-            def send():
-                return pltpu.make_async_remote_copy(
-                    src_ref=source(block), dst_ref=into.at[axis, slot],
-                    send_sem=S["fin"].at[0, number if i else 4 + number // 2], recv_sem=S["fin"].at[1, number],
-                    device_id=dev, device_id_type=MESH)
-
-            def stay():
-                pltpu.make_async_copy(source(block), into.at[axis, slot], S["fin"].at[1, number]).start()
-
-            if i:
-                send().start()
-            elif axis == 0:
-                stay()
-            else:
-                pl.when(y != z)(lambda: send().start())
-                pl.when(y == z)(stay)
-                ends.append(functools.partial(when_wait, y != z, send()))
-        ends.append(whole(into.at[axis, pl.ds(0, 7)], S["fin"].at[0, number], S["fin"].at[1, number]).wait_send)
-
+    yield "gainsum"
     arrive(blocks)
-    for axis in both:
-        deliver(axis, axis, lambda block: S["ft"].at[block, axis], S["fr"])
+    S["fr"][z] = S["ft"][z]
+    owned = spread("fr", z, 9, "z", lambda i: S["ft"].at[(z + i) % 8])
+    yield "deliver1"
     arrive(gains)
-    for axis in both:
-        deliver(2 + axis, axis, lambda block: S["gs"].at[block], S["gr"])
+    S["gr"][z] = S["gs"][z]
+    gain_parts = spread("gr", z, 10, "z", lambda i: S["gs"].at[(z + i) % 8])
+    yield "deliver2"
     gcol = turned(S["gown"][0:1])[:F]
     mean, inv = scale_of(S["stc"][d])
     cen = (x_ref[...].astype(f32) - mean) * inv
     tile = jnp.sum(S["s2z"][...], axis=0)
     base = t_ref[...].astype(f32) - inv * (tile[0:1] / D + cen * (tile[1:2] / D))
-    for axis in both:
-        whole(S["fr"].at[axis], S["fin"].at[0, axis], S["fin"].at[1, axis]).wait_recv()
-    grad = jnp.concatenate([jnp.sum(S["fr"][axis].astype(f32), axis=0) for axis in both], axis=0)
+    arrive(owned)
+    grad = jnp.sum(S["fr"][...].astype(f32), axis=0).reshape(F, 128)
     ig_ref[...] = (base + inv * (grad * gcol)).astype(bf16)
-    for axis in both:
-        whole(S["gr"].at[axis], S["fin"].at[0, 2 + axis], S["fin"].at[1, 2 + axis]).wait_recv()
-    lane = lax.broadcasted_iota(jnp.int32, (8, 128), 1)
-    gg_out[...] = jnp.where(lane < HALF, jnp.sum(S["gr"][0], axis=0), jnp.sum(S["gr"][1], axis=0))
+    arrive(gain_parts)
+    yield "final"
+    gg_out[...] = jnp.sum(S["gr"][...], axis=0)
+
+
+def hand_over(*refs):
+    ins, outs, sem = refs[:4], refs[4:8], refs[8]
+    copies = [pltpu.make_async_copy(ins[i], outs[i], sem.at[i]) for i in (0, 1)]
+    for copy in copies:
+        copy.start()
+    outs[2][...] = ins[2][...]
+    outs[3][...] = ins[3][0:1, :F]
+    for copy in copies:
+        copy.wait()
 
 
 def shards(inputs, gain, w_in, w_out, targets):
@@ -496,7 +480,19 @@
         cost_estimate=pl.CostEstimate(flops=2 * 10 ** 9, bytes_accessed=4 * 10 ** 6, transcendentals=10 ** 5),
         name="backward",
     )(inputs.T, targets.T, gain.reshape(1, F), w_in, w_out)
-    return input_grad.T, gain_grad[0, :F], w_in_grad, w_out_grad
+    w_in_grad, w_out_grad, input_grad, gain_grad = pl.pallas_call(
+        hand_over,
+        out_shape=(
+            jax.ShapeDtypeStruct((K, H), f32), jax.ShapeDtypeStruct((H, K), f32),
+            jax.ShapeDtypeStruct((F, 128), bf16), jax.ShapeDtypeStruct((1, F), f32)),
+        in_specs=[hbm, hbm, vmem, vmem],
+        out_specs=(hbm, hbm, vmem, vmem),
+        scratch_shapes=[pltpu.SemaphoreType.DMA((2,))],
+        compiler_params=pltpu.CompilerParams(vmem_limit_bytes=60 * 1024 * 1024),
+        cost_estimate=pl.CostEstimate(flops=0, bytes_accessed=3 * 10 ** 6, transcendentals=0),
+        name="hand_over",
+    )(w_in_grad, w_out_grad, input_grad, gain_grad)
+    return input_grad.T, gain_grad.reshape(F), w_in_grad, w_out_grad
 
 
 def solution(mesh):

time: 109 us -> 149 us (1.37)
  Pallas kernels: 101 us -> 148 us
  local copies, waits for them, and re-layouts: 5.55 us -> 0 us
    pallas_call x0 -> x1, Pallas kernels: none -> 50.1 us  [shards(): pl.pallas_call(hand_over, out_shape=(jax.ShapeDtypeStruct((K, H), f32), j...]
    unnamed x5 -> x0, local copies, waits for them, and re-layouts: 4.36 us -> none
    pallas_call x1, Pallas kernels: 101 us -> 97.8 us  [shards(): pl.pallas_call(kernel, out_shape=(jax.ShapeDtypeStruct((F, 128), bf16), j...]
where the time goes in v4:
time: 149 us
  Pallas kernels  148 us (99%)
    pallas_call x1, Pallas kernels, shards(): pl.pallas_call(kernel, out_shape=(jax.ShapeDtypeStruct((F, 128), bf16), j...  97.8 us
    pallas_call x1, Pallas kernels, shards(): pl.pallas_call(hand_over, out_shape=(jax.ShapeDtypeStruct((K, H), f32), j...  50.1 us

profile of v4, /device:TPU:1, one launch (start us, length us, event | category | flops | bytes accessed | tf_op | source)
XLA Modules:
  0.0 148.6 jit_solution(18011665599180766897)
XLA Ops:
  0.6 97.8 %backward.1 = (bf16[96,128]{1,0:T(8,128)(2,1)}, f32[8,128]{1,0:T(8,128)}, f32[768,256]{1,0:T(8,128)}, f32[256,768]{1,0:T(8,128)}) custom-call(bf16[96,128]{1,0:T(8,128)(2,1)} %bitcast.5, bf16[96,128]{1,0:T(8,128)(2,1)} %bitcast.6, bf16[1,96]{1,0:T(2,128)(2,1)} %bitcast.8, bf16[768,256]{1,0:T(8,128)(2,1)} %refs_3_.1, bf16[256,768]{1,0:T(8,128)(2,1)} %refs_4_.1), custom_call_target="tpu_custom_call" | custom-call | flops 2000000000 | bytes 4000000 | tf_op jit(solution)/shard_map/backward/pallas_call | solution.py:470
  98.4 50.1 %hand_over.1 = (f32[768,256]{1,0:T(8,128)}, f32[256,768]{1,0:T(8,128)}, bf16[96,128]{1,0:T(8,128)(2,1)}, f32[1,96]{1,0:T(1,128)}) custom-call(f32[768,256]{1,0:T(8,128)} %get-tuple-element.12.refs_0_, f32[256,768]{1,0:T(8,128)} %get-tuple-element.13.refs_1_, bf16[96,128]{1,0:T(8,128)(2,1)} %get-tuple-element.14.refs_2_, f32[8,128]{1,0:T(8,128)} %get-tuple-element.15.refs_3_), custom_call_target="tpu_custom_call" | custom-call | bytes 3000000 | tf_op jit(solution)/shard_map/hand_over/pallas_call | solution.py:483

commit v5 on v4

--- a/solution.py
+++ b/solution.py
@@ -163,15 +163,16 @@
     arrive(perm)
     yield "permute"
 
-    gx = [
-        go(S["xg"].at[z, y], S["xg"].at[z, y], "sx", (i - 1,), along("z", i)) for i in range(1, 8)]
-    gt = [go(S["tg"].at[z, y], S["tg"].at[z, y], "stg", (i - 1,), along("y", i)) for i in range(1, 8)]
     ggain = spread("gg", y, 0, "y")
     piece = S["xg"][z, y].astype(f32)
     S["sta"][y] = jnp.zeros((8, 128), f32)
     S["sta"][y, 0:1] = jnp.sum(piece, axis=0, keepdims=True)
     S["sta"][y, 1:2] = jnp.sum(piece * piece, axis=0, keepdims=True)
     sta = spread("sta", y, 1, "y")
+
+    gx = [
+        go(S["xg"].at[z, y], S["xg"].at[z, y], "sx", (i - 1,), along("z", i)) for i in range(1, 8)]
+    gt = [go(S["tg"].at[z, y], S["tg"].at[z, y], "stg", (i - 1,), along("y", i)) for i in range(1, 8)]
     def offset(e):
         return (e + 1) // 2 if e % 2 else (8 - e // 2) % 8
 
@@ -226,6 +227,13 @@
     arrive(sta)
     S["stb"][d] = jnp.sum(S["sta"][...], axis=0)
     stb = spread("stb", d, 2, "dp")
+    lax.fori_loop(0, 4, functools.partial(ring_rest, 2), 0)
+    yield "ring2"
+    arrive(stb)
+    S["stc"][z] = jnp.sum(S["stb"][...], axis=0)
+    stc = spread("stc", z, 3, "z")
+    lax.fori_loop(0, 4, functools.partial(ring_rest, 3), 0)
+    yield "ring3"
     arrive(ggain)
     for load in loads:
         load()
@@ -236,44 +244,38 @@
         S["gb"][i] = turned(rows[0:1])[:F]
         total += jnp.dot(rows[:, :F].astype(bf16), S["w1"][F * i:F * (i + 1)], preferred_element_type=f32)
     S["u"][...] = total
-    lax.fori_loop(0, 4, functools.partial(ring_rest, 2), 0)
-    yield "ring2"
-    arrive(stb)
-    S["stc"][z] = jnp.sum(S["stb"][...], axis=0)
-    stc = spread("stc", z, 3, "z")
-    lax.fori_loop(0, 4, functools.partial(ring_rest, 3), 0)
-    yield "ring3"
     arrive(stc)
     lax.fori_loop(0, 2, ring_last, 0)
-    for axis in (0, 1):
-        for way in (0, 1):
-            for j in (0, 1):
-                ring_wait(axis, way, 3, 2 * j + 1 - way)
-                ring_wait(axis, way, 4, 2 * j + way)
-    yield "ring"
+    for way in (0, 1):
+        ring_wait(0, way, 3, 1 - way)
+        ring_wait(0, way, 4, way)
+    yield "ringhalf"
+
+    place = [(z + offset(e)) % 8 for e in range(8)]
 
     def scale_of(tile):
         mean = tile[0:1] / D
         return mean, lax.rsqrt(tile[1:2] / D - mean * mean + epsilon)
 
-    def normed(tok, carry):
-        mean, inv = scale_of(S["stc"][tok])
-        for i in range(8):
-            S["nt"][tok, i] = ((S["xg"][tok, i].astype(f32) - mean) * inv * S["gb"][i]).astype(bf16)
-        return carry
-
-    lax.fori_loop(0, 8, normed, 0)
-
-    def pair(ref, i):
-        return jnp.concatenate(
-            [ref[2 * i].reshape(K, 128), ref[2 * i + 1].reshape(K, 128)], axis=1)
+    def normed(h):
+        for e in range(4 * h, 4 * h + 4):
+            mean, inv = scale_of(S["stc"][place[e]])
+
+            def rows(i, carry):
+                S["nt"][e, i] = ((S["xg"][place[e], i].astype(f32) - mean) * inv * S["gb"][i]).astype(bf16)
+                return carry
+
+            lax.fori_loop(0, 8, rows, 0)
+
+    def joined(ref, spots):
+        return jnp.concatenate([ref[i].reshape(K, 128) for i in spots], axis=1)
 
     def products(h):
         for i in (2 * h, 2 * h + 1):
             lanes = slice(256 * (i % 2), 256 * (i % 2 + 1))
             pre_part = lax.dot_general(
-                S["w1"][...], pair(S["nt"], i), (((0,), (0,)), ((), ())), preferred_element_type=f32)
-            act_part = jnp.dot(S["w2"][...], pair(S["tg"], i), preferred_element_type=f32)
+                S["w1"][...], joined(S["nt"], (2 * i, 2 * i + 1)), (((0,), (0,)), ((), ())), preferred_element_type=f32)
+            act_part = jnp.dot(S["w2"][...], joined(S["tg"], place[2 * i:2 * i + 2]), preferred_element_type=f32)
             S["part"][h, 0, :, :, :, lanes] = pre_part.reshape(4, 2, Q, 256)
             S["part"][h, 1, :, :, :, lanes] = act_part.reshape(4, 2, Q, 256)
         pairs = {}
@@ -310,8 +312,8 @@
             for i in (1, 2, 3)}
         second = jnp.sum(pre_grad.astype(f32) * pre_act, axis=0, keepdims=True)
         for i in range(4):
-            S["s2p"][4 * h + i] = jnp.zeros((8, 128), f32)
-            S["s2p"][4 * h + i, 1:2] = second[:, 128 * i:128 * (i + 1)]
+            S["s2p"][place[4 * h + i]] = jnp.zeros((8, 128), f32)
+            S["s2p"][place[4 * h + i], 1:2] = second[:, 128 * i:128 * (i + 1)]
         return hops
 
     def pass_on(h, hops):
@@ -325,9 +327,18 @@
         return pairs
 
     both = (0, 1)
-    pairs = [products(h) for h in both]
-    yield "products"
-    hops = [chip_sum(h, pairs[h]) for h in both]
+    normed(0)
+    pairs = {0: products(0)}
+    hops = {0: chip_sum(0, pairs[0])}
+    for way in both:
+        ring_wait(0, way, 3, 3 - way)
+        ring_wait(0, way, 4, 2 + way)
+        for j in both:
+            ring_wait(1, way, 3, 2 * j + 1 - way)
+            ring_wait(1, way, 4, 2 * j + way)
+    normed(1)
+    pairs[1] = products(1)
+    hops[1] = chip_sum(1, pairs[1])
     yield "chipsum"
     hops = [activate(h, pairs[h], hops[h]) for h in both]
     yield "dpsum"
@@ -380,13 +391,13 @@
     low = (S["u"][...] - high.astype(f32)).astype(bf16)
     first = jnp.dot(high, pg, preferred_element_type=f32) + jnp.dot(low, pg, preferred_element_type=f32)
     for i in range(8):
-        S["s2p"][i, 0:1] = first[0:1, 128 * i:128 * (i + 1)]
+        S["s2p"][place[i], 0:1] = first[0:1, 128 * i:128 * (i + 1)]
     s2a = spread("s2r", d, 4, "dp", lambda i: S["s2p"].at[(d + i) % 8])
     S["s2r"][d] = S["s2p"][d]
     rs_round(1, 0)
     rs_round(1, 1)
     yield "round1"
-    nt_all = jnp.concatenate([S["nt"][i].reshape(K, 128) for i in range(8)], axis=1)
+    nt_all = joined(S["nt"], range(8))
     S["w1g"][...] = lax.dot_general(nt_all, pg, (((1,), (1,)), ((), ())), preferred_element_type=f32)
     store1 = pltpu.make_async_copy(S["w1g"], w1g_hbm, S["loc"].at[2])
     store1.start()
@@ -398,7 +409,7 @@
     rs_round(2, 0)
     rs_round(2, 1)
     yield "round2"
-    tg_all = jnp.concatenate([S["tg"][i].reshape(K, 128) for i in range(8)], axis=1)
+    tg_all = joined(S["tg"], place)
     S["w2g"][...] = lax.dot_general(act, tg_all, (((1,), (1,)), ((), ())), preferred_element_type=f32)
     store2 = pltpu.make_async_copy(S["w2g"], w2g_hbm, S["loc"].at[3])
     store2.start()
@@ -416,16 +427,17 @@
             val = rs_block(axis, y, h)
             for way in both:
                 val = rs_add(axis, way, 4, h, val)
-            S["ng"][pl.ds(4 * h, 4), y, HALF * axis:HALF * (axis + 1)] = val
-            S["fs"][pl.ds(4 * h, 4), axis] = val.astype(bf16)
+            for i in range(4):
+                S["ng"][4 * h + i, y, HALF * axis:HALF * (axis + 1)] = val[i]
+                S["fs"][place[4 * h + i], axis] = val[i].astype(bf16)
     yield "rings"
 
     S["ft"][d] = S["fs"][d]
     blocks = spread("ft", d, 7, "dp", lambda i: S["fs"].at[(d + i) % 8])
     total = jnp.zeros((F, 128), f32)
     for i in range(8):
-        mean, inv = scale_of(S["stc"][i])
-        total += S["ng"][i, y] * ((S["xg"][i, y].astype(f32) - mean) * inv)
+        mean, inv = scale_of(S["stc"][place[i]])
+        total += S["ng"][i, y] * ((S["xg"][place[i], y].astype(f32) - mean) * inv)
     S["pad"][:F] = total
     S["gs"][d] = jnp.broadcast_to(jnp.sum(S["pad"][...].T, axis=0, keepdims=True), (8, 128))
     gains = spread("gs", d, 8, "dp")
@@ -453,14 +465,24 @@
 
 
 def hand_over(*refs):
-    ins, outs, sem = refs[:4], refs[4:8], refs[8]
-    copies = [pltpu.make_async_copy(ins[i], outs[i], sem.at[i]) for i in (0, 1)]
-    for copy in copies:
-        copy.start()
+    ins, outs, held, sem = refs[:4], refs[4:8], refs[8:10], refs[10]
+    steps = []
+    for i in (0, 1):
+        rows = ins[i].shape[0] // 4
+        for part in range(4):
+            span = pl.ds(rows * part, rows)
+            steps.append((
+                pltpu.make_async_copy(ins[i].at[span], held[i].at[span], sem.at[0, i, part]),
+                pltpu.make_async_copy(held[i].at[span], outs[i].at[span], sem.at[1, i, part])))
+    for load, _ in steps:
+        load.start()
     outs[2][...] = ins[2][...]
     outs[3][...] = ins[3][0:1, :F]
-    for copy in copies:
-        copy.wait()
+    for load, store in steps:
+        load.wait()
+        store.start()
+    for _, store in steps:
+        store.wait()
 
 
 def shards(inputs, gain, w_in, w_out, targets):
@@ -487,7 +509,8 @@
             jax.ShapeDtypeStruct((F, 128), bf16), jax.ShapeDtypeStruct((1, F), f32)),
         in_specs=[hbm, hbm, vmem, vmem],
         out_specs=(hbm, hbm, vmem, vmem),
-        scratch_shapes=[pltpu.SemaphoreType.DMA((2,))],
+        scratch_shapes=[
+            pltpu.VMEM((K, H), f32), pltpu.VMEM((H, K), f32), pltpu.SemaphoreType.DMA((2, 2, 4))],
         compiler_params=pltpu.CompilerParams(vmem_limit_bytes=60 * 1024 * 1024),
         cost_estimate=pl.CostEstimate(flops=0, bytes_accessed=3 * 10 ** 6, transcendentals=0),
         name="hand_over",

time: 149 us -> 101 us (0.68)
  Pallas kernels: 148 us -> 99.6 us
    pallas_call x1, Pallas kernels: 50.1 us -> 3.64 us  [shards(): pl.pallas_call(hand_over, out_shape=(jax.ShapeDtypeStruct((K, H), f32), j...]
    pallas_call x1, Pallas kernels: 97.8 us -> 95.9 us  [shards(): pl.pallas_call(kernel, out_shape=(jax.ShapeDtypeStruct((F, 128), bf16), j...]
where the time goes in v5:
time: 101 us; the launch traced here: 100 us
  Pallas kernels  99.6 us (99%)
    pallas_call x1, Pallas kernels, shards(): pl.pallas_call(kernel, out_shape=(jax.ShapeDtypeStruct((F, 128), bf16), j...  95.9 us
    pallas_call x1, Pallas kernels, shards(): pl.pallas_call(hand_over, out_shape=(jax.ShapeDtypeStruct((K, H), f32), j...  3.64 us

profile of v5, /device:TPU:1, one launch (start us, length us, event | category | flops | bytes accessed | tf_op | source)
XLA Modules:
  0.0 100.2 jit_solution(17378676609735703117)
XLA Ops:
  0.6 95.9 %backward.1 = (bf16[96,128]{1,0:T(8,128)(2,1)}, f32[8,128]{1,0:T(8,128)}, f32[768,256]{1,0:T(8,128)}, f32[256,768]{1,0:T(8,128)}) custom-call(bf16[96,128]{1,0:T(8,128)(2,1)} %bitcast.5, bf16[96,128]{1,0:T(8,128)(2,1)} %bitcast.6, bf16[1,96]{1,0:T(2,128)(2,1)} %bitcast.8, bf16[768,256]{1,0:T(8,128)(2,1)} %refs_3_.1, bf16[256,768]{1,0:T(8,128)(2,1)} %refs_4_.1), custom_call_target="tpu_custom_call" | custom-call | flops 2000000000 | bytes 4000000 | tf_op jit(solution)/shard_map/backward/pallas_call | solution.py:492
  96.6 3.6 %hand_over.1 = (f32[768,256]{1,0:T(8,128)}, f32[256,768]{1,0:T(8,128)}, bf16[96,128]{1,0:T(8,128)(2,1)}, f32[1,96]{1,0:T(1,128)}) custom-call(f32[768,256]{1,0:T(8,128)} %get-tuple-element.12.refs_0_, f32[256,768]{1,0:T(8,128)} %get-tuple-element.13.refs_1_, bf16[96,128]{1,0:T(8,128)(2,1)} %get-tuple-element.14.refs_2_, f32[8,128]{1,0:T(8,128)} %get-tuple-element.15.refs_3_), custom_call_target="tpu_custom_call" | custom-call | bytes 3000000 | tf_op jit(solution)/shard_map/hand_over/pallas_call | solution.py:505

commit v6 on v5

--- a/solution.py
+++ b/solution.py
@@ -30,7 +30,8 @@
 
 SCRATCH = dict(
     w1=((K, H), bf16), w2=((H, K), bf16),
-    pad=((128, 128), f32), gown=((8, 128), f32),
+    pad=((128, 128), f32), xo=((F, 128), bf16), to=((F, 128), bf16), go=((1, F), bf16),
+    igv=((F, 128), bf16), ggv=((1, F), f32), gown=((8, 128), f32),
     xg=((8, 8, F, 128), bf16), tg=((8, 8, F, 128), bf16), nt=((8, 8, F, 128), bf16),
     gg=((8, 8, 128), f32), gb=((8, F, 128), f32),
     sta=((8, 8, 128), f32), stb=((8, 8, 128), f32), stc=((8, 8, 128), f32),
@@ -38,13 +39,13 @@
     xs=((2, 3, 2, Q, 512), bf16), xr=((2, 3, 2, Q, 512), bf16), comb=((2, 8, 2, Q, 512), bf16),
     u=((8, H), f32), s2p=((8, 8, 128), f32), s2r=((8, 8, 128), f32),
     s2y=((8, 8, 128), f32), s2z=((8, 8, 128), f32),
-    ng=((8, 8, F, 128), f32), ra=((2, 2, 4, 8, HALF, 128), bf16), sa=((2, 2, 4, 8, HALF, 128), bf16),
-    fs=((8, 2, HALF, 128), bf16), ft=((8, 2, HALF, 128), bf16), fr=((8, 2, HALF, 128), bf16),
+    ng=((8, 8, F, 128), f32), ra=((2, 4, 2, 8, HALF, 128), bf16), sa=((2, 4, 2, 8, HALF, 128), bf16),
+    fs=((2, 8, HALF, 128), bf16), ft=((2, 8, HALF, 128), bf16), fr=((2, 8, HALF, 128), bf16),
     w1g=((K, H), f32), w2g=((H, K), f32), gs=((8, 8, 128), f32), gr=((8, 8, 128), f32),
 )
 SEMS = dict(
-    loc=(4,), perm=(2, 3), sx=(2, 7), stg=(2, 7), small=(2, 11), ring_s=(2, 4), ring_r=(2, 2, 4, 4),
-    core=(2, 2, 4), xx=(2, 2, 3), ax=(2, 2, 3), ac=(2, 2, 4), rs=(2, 2, 2, 4, 2),
+    loc=(9,), perm=(2, 3), sx=(8,), stg=(8,), small=(2, 13), ring_s=(2, 4), ring_r=(2, 2, 4, 4),
+    core=(2, 2, 4), xx=(2, 2, 3), ax=(2, 2, 3), ac=(2, 2, 4), rs_s=(2, 4), rs_r=(2, 2, 4, 2),
 )
 
 
@@ -56,7 +57,7 @@
         end()
 
 
-def phases(ends, x_ref, t_ref, g_ref, w1_hbm, w2_hbm, ig_ref, gg_out, w1g_hbm, w2g_hbm, *scratch):
+def phases(ends, x_hbm, t_hbm, g_hbm, w1_hbm, w2_hbm, ig_hbm, gg_hbm, w1g_hbm, w2g_hbm, *scratch):
     S = dict(zip(list(SCRATCH) + list(SEMS), scratch, strict=True))
     d, m = lax.axis_index("dp"), lax.axis_index("mp")
     z, y = m // 8, m % 8
@@ -90,41 +91,48 @@
             return at(d, (z + i) % 8, y)
         return at(d, z, (y + i) % 8)
 
-    def spread(buf, slot, number, axis, source=None):
+    def scatter(ref, slot, number, axis, source=None):
         for i in range(1, 8):
-            src = S[buf].at[slot] if source is None else source(i)
-            remote(src, S[buf].at[slot], "small", (number,), along(axis, i)).start()
-        seven = whole(S[buf].at[pl.ds(0, 7)], S["small"].at[0, number], S["small"].at[1, number])
+            src = ref.at[slot] if source is None else source(i)
+            remote(src, ref.at[slot], "small", (number,), along(axis, i)).start()
+        seven = whole(ref.at[pl.ds(0, 7)], S["small"].at[0, number], S["small"].at[1, number])
         ends.append(seven.wait_send)
         return [seven]
+
+    def spread(buf, *rest):
+        return scatter(S[buf], *rest)
 
     def arrive(copies):
         for copy in copies:
             copy.wait_recv()
 
-    load1 = pltpu.make_async_copy(w1_hbm, S["w1"], S["loc"].at[0])
-    load2 = pltpu.make_async_copy(w2_hbm, S["w2"], S["loc"].at[1])
-    load1.start()
-    load2.start()
-    loads = [load1.wait, load2.wait]
+    def local(src, dst, number):
+        copy = pltpu.make_async_copy(src, dst, S["loc"].at[number])
+        copy.start()
+        return copy
+
+    small_loads = [local(ref, S[name], i) for i, (ref, name) in enumerate(((x_hbm, "xo"), (t_hbm, "to"), (g_hbm, "go")))]
+    loads = [local(w1_hbm, S["w1"], 3).wait, local(w2_hbm, S["w2"], 4).wait]
     ends.extend(loads)
 
     barrier = pltpu.get_barrier_semaphore()
 
     def hail(dev):
         pl.semaphore_signal(barrier, inc=1, device_id=dev, device_id_type=MESH)
-
-    for axis in ("dp", "z", "y"):
-        for i in range(1, 8):
-            hail(along(axis, i))
 
     @pl.when(off_diag)
     def _():
         hail(at(z, d, y))
 
+    for axis in ("z", "y", "dp"):
+        for i in (4, 3, 5, 2, 6, 1, 7):
+            hail(along(axis, i))
+
     S["pad"][...] = jnp.zeros_like(S["pad"])
     S["gown"][...] = jnp.zeros_like(S["gown"])
-    S["gown"][:, :F] = jnp.broadcast_to(g_ref[...].astype(f32), (8, F))
+    for load in small_loads:
+        load.wait()
+    S["gown"][:, :F] = jnp.broadcast_to(S["go"][...].astype(f32), (8, F))
 
     @pl.when(off_diag)
     def _():
@@ -136,8 +144,8 @@
 
     yield "barrier"
     perm = [
-        (x_ref, S["xg"].at[d, y]),
-        (t_ref, S["tg"].at[d, y]),
+        (S["xo"], S["xg"].at[d, y]),
+        (S["to"], S["tg"].at[d, y]),
         (S["gown"], S["gg"].at[y]),
     ]
     perm = [remote(src, dst, "perm", (i,), at(z, d, y)) for i, (src, dst) in enumerate(perm)]
@@ -149,8 +157,8 @@
 
     @pl.when(diag)
     def _():
-        pltpu.make_async_copy(x_ref, S["xg"].at[z, y], S["perm"].at[1, 0]).start()
-        pltpu.make_async_copy(t_ref, S["tg"].at[z, y], S["perm"].at[1, 1]).start()
+        pltpu.make_async_copy(S["xo"], S["xg"].at[z, y], S["perm"].at[1, 0]).start()
+        pltpu.make_async_copy(S["to"], S["tg"].at[z, y], S["perm"].at[1, 1]).start()
         pltpu.make_async_copy(S["gown"], S["gg"].at[y], S["perm"].at[1, 2]).start()
 
     @ends.append
@@ -160,19 +168,29 @@
             for copy in perm:
                 copy.wait_send()
 
-    arrive(perm)
-    yield "permute"
-
-    ggain = spread("gg", y, 0, "y")
+    def first_stage(ref, sem, axis):
+        copies = [
+            pltpu.make_async_remote_copy(
+                src_ref=ref.at[z, y], dst_ref=ref.at[z, y], send_sem=S[sem].at[7], recv_sem=S[sem].at[i - 1],
+                device_id=along(axis, i), device_id_type=MESH) for i in range(1, 8)]
+        for copy in (copies[i] for i in (3, 2, 4, 1, 5, 0, 6)):
+            copy.start()
+        ends.append(whole(ref.at[0, pl.ds(0, 7)], S[sem].at[7], S[sem].at[0]).wait_send)
+        return copies
+
+    perm[0].wait_recv()
+    gx = first_stage(S["xg"], "sx", "z")
     piece = S["xg"][z, y].astype(f32)
     S["sta"][y] = jnp.zeros((8, 128), f32)
     S["sta"][y, 0:1] = jnp.sum(piece, axis=0, keepdims=True)
     S["sta"][y, 1:2] = jnp.sum(piece * piece, axis=0, keepdims=True)
+    perm[1].wait_recv()
+    gt = first_stage(S["tg"], "stg", "y")
     sta = spread("sta", y, 1, "y")
-
-    gx = [
-        go(S["xg"].at[z, y], S["xg"].at[z, y], "sx", (i - 1,), along("z", i)) for i in range(1, 8)]
-    gt = [go(S["tg"].at[z, y], S["tg"].at[z, y], "stg", (i - 1,), along("y", i)) for i in range(1, 8)]
+    perm[2].wait_recv()
+    ggain = spread("gg", y, 0, "y")
+    yield "permute"
+
     def offset(e):
         return (e + 1) // 2 if e % 2 else (8 - e // 2) % 8
 
@@ -361,7 +379,7 @@
     def rs_add(axis, way, k, h, val):
         if (axis, way, k, h) in rs:
             rs[axis, way, k, h].wait_recv()
-            val = val + S["ra"][axis, way, k - 1, pl.ds(4 * h, 4)].astype(f32)
+            val = val + S["ra"][axis, k - 1, way, pl.ds(4 * h, 4)].astype(f32)
         return val
 
     def rs_round(r, h):
@@ -374,10 +392,12 @@
                 val = rs_block(axis, (y + sign * (5 - k) + 8) % 8, h)
                 val = rs_add(axis, way, k - 1, h, val)
                 half = pl.ds(4 * h, 4)
-                S["sa"][axis, way, k - 1, half] = val.astype(bf16)
-                rs[axis, way, k, h] = go(
-                    S["sa"].at[axis, way, k - 1, half], S["ra"].at[axis, way, k - 1, half],
-                    "rs", (axis, way, k - 1, h), along("y", sign + 8))
+                S["sa"][axis, k - 1, way, half] = val.astype(bf16)
+                rs[axis, way, k, h] = pltpu.make_async_remote_copy(
+                    src_ref=S["sa"].at[axis, k - 1, way, half], dst_ref=S["ra"].at[axis, k - 1, way, half],
+                    send_sem=S["rs_s"].at[axis, k - 1], recv_sem=S["rs_r"].at[axis, way, k - 1, h],
+                    device_id=along("y", sign + 8), device_id_type=MESH)
+                rs[axis, way, k, h].start()
 
     yield "passon"
     norm_products(0)
@@ -385,8 +405,10 @@
     norm_products(1)
     yield "dpgather"
     rs_round(0, 1)
-    pg, act = (
-        jnp.concatenate([S["comb"][h, :, arr].reshape(H, 512) for h in both], axis=1) for arr in (1, 0))
+    def hidden(arr):
+        return jnp.concatenate([S["comb"][h, :, arr].reshape(H, 512) for h in both], axis=1)
+
+    pg = hidden(1)
     high = S["u"][...].astype(bf16)
     low = (S["u"][...] - high.astype(f32)).astype(bf16)
     first = jnp.dot(high, pg, preferred_element_type=f32) + jnp.dot(low, pg, preferred_element_type=f32)
@@ -396,25 +418,11 @@
     S["s2r"][d] = S["s2p"][d]
     rs_round(1, 0)
     rs_round(1, 1)
-    yield "round1"
-    nt_all = joined(S["nt"], range(8))
-    S["w1g"][...] = lax.dot_general(nt_all, pg, (((1,), (1,)), ((), ())), preferred_element_type=f32)
-    store1 = pltpu.make_async_copy(S["w1g"], w1g_hbm, S["loc"].at[2])
-    store1.start()
-    ends.append(store1.wait)
-    yield "w1g"
     arrive(s2a)
     S["s2y"][y] = jnp.sum(S["s2r"][...], axis=0)
     s2b = spread("s2y", y, 5, "y")
     rs_round(2, 0)
     rs_round(2, 1)
-    yield "round2"
-    tg_all = joined(S["tg"], place)
-    S["w2g"][...] = lax.dot_general(act, tg_all, (((1,), (1,)), ((), ())), preferred_element_type=f32)
-    store2 = pltpu.make_async_copy(S["w2g"], w2g_hbm, S["loc"].at[3])
-    store2.start()
-    ends.append(store2.wait)
-    yield "w2g"
     arrive(s2b)
     S["s2z"][z] = jnp.sum(S["s2y"][...], axis=0)
     s2c = spread("s2z", z, 6, "z")
@@ -423,61 +431,75 @@
     yield "round3"
     arrive(s2c)
     for axis in both:
+        for k in (1, 2, 3, 4):
+            ends.append(whole(
+                S["sa"].at[axis, k - 1, 0] if k == 1 else S["sa"].at[axis, k - 1],
+                S["rs_s"].at[axis, k - 1], S["rs_r"].at[axis, 0, 0, 0]).wait_send)
+
+    def parts(axis):
         for h in both:
             val = rs_block(axis, y, h)
             for way in both:
                 val = rs_add(axis, way, 4, h, val)
             for i in range(4):
                 S["ng"][4 * h + i, y, HALF * axis:HALF * (axis + 1)] = val[i]
-                S["fs"][place[4 * h + i], axis] = val[i].astype(bf16)
+                S["fs"][axis, place[4 * h + i]] = val[i].astype(bf16)
+        S["ft"][axis, d] = S["fs"][axis, d]
+        return scatter(S["ft"].at[axis], d, 7 + axis, "dp", lambda i: S["fs"].at[axis, (d + i) % 8])
+
+    def to_owners(axis):
+        S["fr"][axis, z] = S["ft"][axis, z]
+        return scatter(S["fr"].at[axis], z, 9 + axis, "z", lambda i: S["ft"].at[axis, (z + i) % 8])
+
+    blocks = [parts(axis) for axis in both]
     yield "rings"
-
-    S["ft"][d] = S["fs"][d]
-    blocks = spread("ft", d, 7, "dp", lambda i: S["fs"].at[(d + i) % 8])
     total = jnp.zeros((F, 128), f32)
     for i in range(8):
         mean, inv = scale_of(S["stc"][place[i]])
         total += S["ng"][i, y] * ((S["xg"][place[i], y].astype(f32) - mean) * inv)
     S["pad"][:F] = total
     S["gs"][d] = jnp.broadcast_to(jnp.sum(S["pad"][...].T, axis=0, keepdims=True), (8, 128))
-    gains = spread("gs", d, 8, "dp")
-
-    yield "gainsum"
-    arrive(blocks)
-    S["fr"][z] = S["ft"][z]
-    owned = spread("fr", z, 9, "z", lambda i: S["ft"].at[(z + i) % 8])
-    yield "deliver1"
+    gains = spread("gs", d, 11, "dp")
+    arrive(blocks[0])
+    owned = [to_owners(0)]
+    arrive(blocks[1])
+    owned.append(to_owners(1))
     arrive(gains)
     S["gr"][z] = S["gs"][z]
-    gain_parts = spread("gr", z, 10, "z", lambda i: S["gs"].at[(z + i) % 8])
-    yield "deliver2"
+    gain_parts = spread("gr", z, 12, "z", lambda i: S["gs"].at[(z + i) % 8])
+    nt_all = joined(S["nt"], range(8))
+    S["w1g"][...] = lax.dot_general(nt_all, hidden(1), (((1,), (1,)), ((), ())), preferred_element_type=f32)
+    ends.append(local(S["w1g"], w1g_hbm, 5).wait)
+    tg_all = joined(S["tg"], place)
+    S["w2g"][...] = lax.dot_general(hidden(0), tg_all, (((1,), (1,)), ((), ())), preferred_element_type=f32)
+    ends.append(local(S["w2g"], w2g_hbm, 6).wait)
     gcol = turned(S["gown"][0:1])[:F]
     mean, inv = scale_of(S["stc"][d])
-    cen = (x_ref[...].astype(f32) - mean) * inv
+    cen = (S["xo"][...].astype(f32) - mean) * inv
     tile = jnp.sum(S["s2z"][...], axis=0)
-    base = t_ref[...].astype(f32) - inv * (tile[0:1] / D + cen * (tile[1:2] / D))
-    arrive(owned)
-    grad = jnp.sum(S["fr"][...].astype(f32), axis=0).reshape(F, 128)
-    ig_ref[...] = (base + inv * (grad * gcol)).astype(bf16)
+    base = S["to"][...].astype(f32) - inv * (tile[0:1] / D + cen * (tile[1:2] / D))
+    for axis in both:
+        arrive(owned[axis])
+    grad = jnp.concatenate([jnp.sum(S["fr"][axis].astype(f32), axis=0) for axis in both], axis=0)
+    S["igv"][...] = (base + inv * (grad * gcol)).astype(bf16)
+    ends.append(local(S["igv"], ig_hbm, 7).wait)
     arrive(gain_parts)
-    yield "final"
-    gg_out[...] = jnp.sum(S["gr"][...], axis=0)
+    S["ggv"][...] = jnp.sum(S["gr"][...], axis=0)[0:1, :F]
+    ends.append(local(S["ggv"], gg_hbm, 8).wait)
 
 
 def hand_over(*refs):
-    ins, outs, held, sem = refs[:4], refs[4:8], refs[8:10], refs[10]
+    ins, outs, held, sem = refs[:4], refs[4:8], refs[8:12], refs[12]
     steps = []
-    for i in (0, 1):
+    for i in (2, 3, 0, 1):
         rows = ins[i].shape[0] // 4
-        for part in range(4):
-            span = pl.ds(rows * part, rows)
+        for part in range(4 if i < 2 else 1):
+            span = pl.ds(rows * part, rows) if i < 2 else slice(None)
             steps.append((
                 pltpu.make_async_copy(ins[i].at[span], held[i].at[span], sem.at[0, i, part]),
                 pltpu.make_async_copy(held[i].at[span], outs[i].at[span], sem.at[1, i, part])))
     for load, _ in steps:
         load.start()
-    outs[2][...] = ins[2][...]
-    outs[3][...] = ins[3][0:1, :F]
     for load, store in steps:
         load.wait()
         store.start()
@@ -486,16 +508,17 @@
 
 
 def shards(inputs, gain, w_in, w_out, targets):
-    vmem, hbm = pl.BlockSpec(memory_space=pltpu.VMEM), pl.BlockSpec(memory_space=pl.ANY)
+    hbm = pl.BlockSpec(memory_space=pl.ANY)
     scratch = [pltpu.VMEM(shape, kind) for shape, kind in SCRATCH.values()]
     scratch += [pltpu.SemaphoreType.DMA(shape) for shape in SEMS.values()]
+    results = (
+        jax.ShapeDtypeStruct((K, H), f32), jax.ShapeDtypeStruct((H, K), f32),
+        jax.ShapeDtypeStruct((F, 128), bf16), jax.ShapeDtypeStruct((1, F), f32))
     input_grad, gain_grad, w_in_grad, w_out_grad = pl.pallas_call(
         kernel,
-        out_shape=(
-            jax.ShapeDtypeStruct((F, 128), bf16), jax.ShapeDtypeStruct((8, 128), f32),
-            jax.ShapeDtypeStruct((K, H), f32), jax.ShapeDtypeStruct((H, K), f32)),
-        in_specs=[vmem, vmem, vmem, hbm, hbm],
-        out_specs=(vmem, vmem, hbm, hbm),
+        out_shape=(*results[2:], *results[:2]),
+        in_specs=[hbm] * 5,
+        out_specs=(hbm,) * 4,
         scratch_shapes=scratch,
         compiler_params=pltpu.CompilerParams(
             collective_id=0, has_side_effects=True, vmem_limit_bytes=60 * 1024 * 1024),
@@ -504,13 +527,10 @@
     )(inputs.T, targets.T, gain.reshape(1, F), w_in, w_out)
     w_in_grad, w_out_grad, input_grad, gain_grad = pl.pallas_call(
         hand_over,
-        out_shape=(
-            jax.ShapeDtypeStruct((K, H), f32), jax.ShapeDtypeStruct((H, K), f32),
-            jax.ShapeDtypeStruct((F, 128), bf16), jax.ShapeDtypeStruct((1, F), f32)),
-        in_specs=[hbm, hbm, vmem, vmem],
-        out_specs=(hbm, hbm, vmem, vmem),
-        scratch_shapes=[
-            pltpu.VMEM((K, H), f32), pltpu.VMEM((H, K), f32), pltpu.SemaphoreType.DMA((2, 2, 4))],
+        out_shape=results,
+        in_specs=[hbm] * 4,
+        out_specs=(hbm,) * 4,
+        scratch_shapes=[pltpu.VMEM(out.shape, out.dtype) for out in results] + [pltpu.SemaphoreType.DMA((2, 4, 4))],
         compiler_params=pltpu.CompilerParams(vmem_limit_bytes=60 * 1024 * 1024),
         cost_estimate=pl.CostEstimate(flops=0, bytes_accessed=3 * 10 ** 6, transcendentals=0),
         name="hand_over",

time: 101 us -> 96.8 us (0.958)
  Pallas kernels: 99.6 us -> 95.9 us
    pallas_call x2, Pallas kernels: 99.6 us -> 95.9 us  [the longest x1 93.5 us: shards(): pl.pallas_call(kernel, out_shape=(*results[2:], *results[:2]), in_specs=[...]
where the time goes in v6:
time: 96.8 us; the launch traced here: 96.6 us
  Pallas kernels  95.9 us (99%)
    pallas_call x1, Pallas kernels, shards(): pl.pallas_call(kernel, out_shape=(*results[2:], *results[:2]), in_specs=[...  93.5 us
    pallas_call x1, Pallas kernels, shards(): pl.pallas_call(hand_over, out_shape=results, in_specs=[hbm] * 4, out_spec...  2.45 us

profile of v6, /device:TPU:1, one launch (start us, length us, event | category | flops | bytes accessed | tf_op | source)
XLA Modules:
  0.0 96.6 jit_solution(636765069810629828)
XLA Ops:
  0.6 93.5 %backward.1 = (bf16[96,128]{1,0:T(8,128)(2,1)}, f32[1,96]{1,0:T(1,128)}, f32[768,256]{1,0:T(8,128)}, f32[256,768]{1,0:T(8,128)}) custom-call(bf16[96,128]{1,0:T(8,128)(2,1)} %bitcast.5, bf16[96,128]{1,0:T(8,128)(2,1)} %bitcast.6, bf16[1,96]{1,0:T(2,128)(2,1)} %bitcast.8, bf16[768,256]{1,0:T(8,128)(2,1)} %refs_3_.1, bf16[256,768]{1,0:T(8,128)(2,1)} %refs_4_.1), custom_call_target="tpu_custom_call" | custom-call | flops 2000000000 | bytes 4000000 | tf_op jit(solution)/shard_map/backward/pallas_call | solution.py:517
  94.1 2.5 %hand_over.1 = (f32[768,256]{1,0:T(8,128)}, f32[256,768]{1,0:T(8,128)}, bf16[96,128]{1,0:T(8,128)(2,1)}, f32[1,96]{1,0:T(1,128)}) custom-call(f32[768,256]{1,0:T(8,128)} %get-tuple-element.12.refs_0_, f32[256,768]{1,0:T(8,128)} %get-tuple-element.13.refs_1_, bf16[96,128]{1,0:T(8,128)(2,1)} %get-tuple-element.14.refs_2_, f32[1,96]{1,0:T(1,128)} %get-tuple-element.15.refs_3_), custom_call_target="tpu_custom_call" | custom-call | bytes 3000000 | tf_op jit(solution)/shard_map/hand_over/pallas_call | solution.py:528

commit v7 on v6

--- a/solution.py
+++ b/solution.py
@@ -173,19 +173,19 @@
             pltpu.make_async_remote_copy(
                 src_ref=ref.at[z, y], dst_ref=ref.at[z, y], send_sem=S[sem].at[7], recv_sem=S[sem].at[i - 1],
                 device_id=along(axis, i), device_id_type=MESH) for i in range(1, 8)]
-        for copy in (copies[i] for i in (3, 2, 4, 1, 5, 0, 6)):
+        for copy in (copies[i] for i in (0, 6, 1, 5, 2, 4, 3)):
             copy.start()
         ends.append(whole(ref.at[0, pl.ds(0, 7)], S[sem].at[7], S[sem].at[0]).wait_send)
         return copies
 
     perm[0].wait_recv()
     gx = first_stage(S["xg"], "sx", "z")
+    perm[1].wait_recv()
+    gt = first_stage(S["tg"], "stg", "y")
     piece = S["xg"][z, y].astype(f32)
     S["sta"][y] = jnp.zeros((8, 128), f32)
     S["sta"][y, 0:1] = jnp.sum(piece, axis=0, keepdims=True)
     S["sta"][y, 1:2] = jnp.sum(piece * piece, axis=0, keepdims=True)
-    perm[1].wait_recv()
-    gt = first_stage(S["tg"], "stg", "y")
     sta = spread("sta", y, 1, "y")
     perm[2].wait_recv()
     ggain = spread("gg", y, 0, "y")
@@ -231,6 +231,10 @@
         return carry
 
     for e in range(8):
+        if e == 6:
+            arrive(sta)
+            S["stb"][d] = jnp.sum(S["sta"][...], axis=0)
+            stb = spread("stb", d, 2, "dp")
         for axis in (0, 1):
             if e:
                 (gx, gt)[axis][7 - offset(e)].wait_recv()
@@ -241,17 +245,13 @@
             ends.append(whole(
                 S["xg"].at[pl.ds(0, 2)] if k < 4 else S["xg"].at[0],
                 S["ring_s"].at[axis, k - 1], S["ring_r"].at[axis, 0, 0, 0]).wait_send)
-    yield "ring1"
-    arrive(sta)
-    S["stb"][d] = jnp.sum(S["sta"][...], axis=0)
-    stb = spread("stb", d, 2, "dp")
     lax.fori_loop(0, 4, functools.partial(ring_rest, 2), 0)
     yield "ring2"
     arrive(stb)
     S["stc"][z] = jnp.sum(S["stb"][...], axis=0)
     stc = spread("stc", z, 3, "z")
     lax.fori_loop(0, 4, functools.partial(ring_rest, 3), 0)
-    yield "ring3"
+    lax.fori_loop(0, 2, ring_last, 0)
     arrive(ggain)
     for load in loads:
         load()
@@ -263,7 +263,6 @@
         total += jnp.dot(rows[:, :F].astype(bf16), S["w1"][F * i:F * (i + 1)], preferred_element_type=f32)
     S["u"][...] = total
     arrive(stc)
-    lax.fori_loop(0, 2, ring_last, 0)
     for way in (0, 1):
         ring_wait(0, way, 3, 1 - way)
         ring_wait(0, way, 4, way)
@@ -420,16 +419,11 @@
     rs_round(1, 1)
     arrive(s2a)
     S["s2y"][y] = jnp.sum(S["s2r"][...], axis=0)
-    s2b = spread("s2y", y, 5, "y")
     rs_round(2, 0)
     rs_round(2, 1)
-    arrive(s2b)
-    S["s2z"][z] = jnp.sum(S["s2y"][...], axis=0)
-    s2c = spread("s2z", z, 6, "z")
+    s2b = spread("s2y", y, 5, "y")
     rs_round(3, 0)
     rs_round(3, 1)
-    yield "round3"
-    arrive(s2c)
     for axis in both:
         for k in (1, 2, 3, 4):
             ends.append(whole(
@@ -460,6 +454,8 @@
     S["pad"][:F] = total
     S["gs"][d] = jnp.broadcast_to(jnp.sum(S["pad"][...].T, axis=0, keepdims=True), (8, 128))
     gains = spread("gs", d, 11, "dp")
+    arrive(s2b)
+    S["s2z"][z] = jnp.sum(S["s2y"][...], axis=0)
     arrive(blocks[0])
     owned = [to_owners(0)]
     arrive(blocks[1])
@@ -467,6 +463,7 @@
     arrive(gains)
     S["gr"][z] = S["gs"][z]
     gain_parts = spread("gr", z, 12, "z", lambda i: S["gs"].at[(z + i) % 8])
+    s2c = spread("s2z", z, 6, "z")
     nt_all = joined(S["nt"], range(8))
     S["w1g"][...] = lax.dot_general(nt_all, hidden(1), (((1,), (1,)), ((), ())), preferred_element_type=f32)
     ends.append(local(S["w1g"], w1g_hbm, 5).wait)
@@ -476,6 +473,7 @@
     gcol = turned(S["gown"][0:1])[:F]
     mean, inv = scale_of(S["stc"][d])
     cen = (S["xo"][...].astype(f32) - mean) * inv
+    arrive(s2c)
     tile = jnp.sum(S["s2z"][...], axis=0)
     base = S["to"][...].astype(f32) - inv * (tile[0:1] / D + cen * (tile[1:2] / D))
     for axis in both:

time: 96.8 us -> 94.9 us (0.980)
  Pallas kernels: 95.9 us -> 94.1 us
    pallas_call x1, Pallas kernels: 93.5 us -> 91.7 us  [shards(): pl.pallas_call(kernel, out_shape=(*results[2:], *results[:2]), in_specs=[...]
where the time goes in v7:
time: 94.9 us; the launch traced here: 94.8 us
  Pallas kernels  94.1 us (99%)
    pallas_call x1, Pallas kernels, shards(): pl.pallas_call(kernel, out_shape=(*results[2:], *results[:2]), in_specs=[...  91.7 us
    pallas_call x1, Pallas kernels, shards(): pl.pallas_call(hand_over, out_shape=results, in_specs=[hbm] * 4, out_spec...  2.45 us

profile of v7, /device:TPU:1, one launch (start us, length us, event | category | flops | bytes accessed | tf_op | source)
XLA Modules:
  0.0 94.8 jit_solution(13899273284336518470)
XLA Ops:
  0.6 91.7 %backward.1 = (bf16[96,128]{1,0:T(8,128)(2,1)}, f32[1,96]{1,0:T(1,128)}, f32[768,256]{1,0:T(8,128)}, f32[256,768]{1,0:T(8,128)}) custom-call(bf16[96,128]{1,0:T(8,128)(2,1)} %bitcast.5, bf16[96,128]{1,0:T(8,128)(2,1)} %bitcast.6, bf16[1,96]{1,0:T(2,128)(2,1)} %bitcast.8, bf16[768,256]{1,0:T(8,128)(2,1)} %refs_3_.1, bf16[256,768]{1,0:T(8,128)(2,1)} %refs_4_.1), custom_call_target="tpu_custom_call" | custom-call | flops 2000000000 | bytes 4000000 | tf_op jit(solution)/shard_map/backward/pallas_call | solution.py:515
  92.3 2.5 %hand_over.1 = (f32[768,256]{1,0:T(8,128)}, f32[256,768]{1,0:T(8,128)}, bf16[96,128]{1,0:T(8,128)(2,1)}, f32[1,96]{1,0:T(1,128)}) custom-call(f32[768,256]{1,0:T(8,128)} %get-tuple-element.12.refs_0_, f32[256,768]{1,0:T(8,128)} %get-tuple-element.13.refs_1_, bf16[96,128]{1,0:T(8,128)(2,1)} %get-tuple-element.14.refs_2_, f32[1,96]{1,0:T(1,128)} %get-tuple-element.15.refs_3_), custom_call_target="tpu_custom_call" | custom-call | bytes 3000000 | tf_op jit(solution)/shard_map/hand_over/pallas_call | solution.py:526

commit v8 on v7

--- a/solution.py
+++ b/solution.py
@@ -456,6 +456,7 @@
     gains = spread("gs", d, 11, "dp")
     arrive(s2b)
     S["s2z"][z] = jnp.sum(S["s2y"][...], axis=0)
+    s2c = spread("s2z", z, 6, "z")
     arrive(blocks[0])
     owned = [to_owners(0)]
     arrive(blocks[1])
@@ -463,7 +464,6 @@
     arrive(gains)
     S["gr"][z] = S["gs"][z]
     gain_parts = spread("gr", z, 12, "z", lambda i: S["gs"].at[(z + i) % 8])
-    s2c = spread("s2z", z, 6, "z")
     nt_all = joined(S["nt"], range(8))
     S["w1g"][...] = lax.dot_general(nt_all, hidden(1), (((1,), (1,)), ((), ())), preferred_element_type=f32)
     ends.append(local(S["w1g"], w1g_hbm, 5).wait)

time: 94.9 us -> 94 us (level)
  no operation moved by 1% of the time
where the time goes in v8:
time: 94 us; the launch traced here: 93.9 us
  Pallas kernels  93.2 us (99%)
    pallas_call x1, Pallas kernels, shards(): pl.pallas_call(kernel, out_shape=(*results[2:], *results[:2]), in_specs=[...  90.8 us
    pallas_call x1, Pallas kernels, shards(): pl.pallas_call(hand_over, out_shape=results, in_specs=[hbm] * 4, out_spec...  2.45 us

profile of v8, /device:TPU:1, one launch (start us, length us, event | category | flops | bytes accessed | tf_op | source)
XLA Modules:
  0.0 93.9 jit_solution(14918295172797062162)
XLA Ops:
  0.6 90.8 %backward.1 = (bf16[96,128]{1,0:T(8,128)(2,1)}, f32[1,96]{1,0:T(1,128)}, f32[768,256]{1,0:T(8,128)}, f32[256,768]{1,0:T(8,128)}) custom-call(bf16[96,128]{1,0:T(8,128)(2,1)} %bitcast.5, bf16[96,128]{1,0:T(8,128)(2,1)} %bitcast.6, bf16[1,96]{1,0:T(2,128)(2,1)} %bitcast.8, bf16[768,256]{1,0:T(8,128)(2,1)} %refs_3_.1, bf16[256,768]{1,0:T(8,128)(2,1)} %refs_4_.1), custom_call_target="tpu_custom_call" | custom-call | flops 2000000000 | bytes 4000000 | tf_op jit(solution)/shard_map/backward/pallas_call | solution.py:515
  91.4 2.5 %hand_over.1 = (f32[768,256]{1,0:T(8,128)}, f32[256,768]{1,0:T(8,128)}, bf16[96,128]{1,0:T(8,128)(2,1)}, f32[1,96]{1,0:T(1,128)}) custom-call(f32[768,256]{1,0:T(8,128)} %get-tuple-element.12.refs_0_, f32[256,768]{1,0:T(8,128)} %get-tuple-element.13.refs_1_, bf16[96,128]{1,0:T(8,128)(2,1)} %get-tuple-element.14.refs_2_, f32[1,96]{1,0:T(1,128)} %get-tuple-element.15.refs_3_), custom_call_target="tpu_custom_call" | custom-call | bytes 3000000 | tf_op jit(solution)/shard_map/hand_over/pallas_call | solution.py:526
